TPU v7x, 256 devices: a whole 4x4x8 slice. The times are simulated.
256 devices in a mesh: chan: 32 (over z, y_lo, core), win: 8 (over y_hi, x).
Axes of the slice: x: 4, y: 4 (y_hi: 2, y_lo: 2; y = y_hi * 2 + y_lo), z: 8, core: 2. Of those that a mesh axis runs over, the one named last changes fastest.
Arguments:
- recordings: bfloat16 [8, 256, 4096], P('win', 'chan'), may hold values from -6 to 6
- channel_live: int32 [256], P('chan'), may hold values 0 or 1
Outputs:
- correlations: float32 [128, 256, 128], P('win', 'chan')
All inputs are finite; a program needn't handle non-finite values. No bound on the sum of `channel_live` on one device may be relied on, other than what follows from the above.
Results may differ from a plain program's by a relative error of at most 0.017.
Values may be sent and summed in bfloat16 or wider, within the bound.
A program may use at most 128 MiB of HBM per device.

v0:
```python
import math

import jax
import jax.numpy as jnp
from jax import lax
from jax.sharding import PartitionSpec as P

WB = 64
BAND = 128
LAGS = 128


def shifted(value, axis, steps):
    count = lax.axis_size(axis)
    leading, last = (max(0, -steps), min(count, count - steps))
    return lax.ppermute(value, axis, [(source, source + steps) for source in range(leading, last)])


def forward_block(samples_flat, first_bin, block_width, sample_count):
    sample_index = lax.broadcasted_iota(jnp.int32, (sample_count, block_width), 0)
    bin_index = lax.broadcasted_iota(jnp.int32, (sample_count, block_width), 1) + first_bin
    angles = (sample_index * bin_index % sample_count).astype(jnp.float32) * (
        2.0 * math.pi / sample_count
    )
    table_block = jnp.concatenate([jnp.cos(angles), -jnp.sin(angles)], axis=1).astype(jnp.bfloat16)
    return jnp.dot(samples_flat, table_block, preferred_element_type=jnp.float32)


def inverse_table(bin_count, sample_count, lag_count, factor):
    bin_index = lax.broadcasted_iota(jnp.int32, (bin_count, lag_count), 0)
    lag_index = lax.broadcasted_iota(jnp.int32, (bin_count, lag_count), 1) - lag_count // 2
    angles = (bin_index * lag_index % sample_count).astype(jnp.float32) * (
        2.0 * math.pi / sample_count
    )
    return jnp.stack([jnp.cos(angles) * factor, -jnp.sin(angles) * factor], axis=0)


def whiten(spec_re, spec_im, channel_live, block_bins):
    leading = spec_re.shape[:-1]
    bin_count = spec_re.shape[-1]
    energy = (spec_re * spec_re + spec_im * spec_im).reshape(
        leading + (bin_count // block_bins, block_bins)
    )
    amplitude = jnp.sqrt(jnp.mean(energy, axis=-1, keepdims=True) + 1e-06)
    inverse_amp = jnp.broadcast_to(1.0 / amplitude, energy.shape).reshape(leading + (bin_count,))
    factor = inverse_amp * channel_live.astype(jnp.float32)[None, :, None]
    return jnp.stack([spec_re * factor, spec_im * factor], axis=2).astype(jnp.bfloat16)


def band_extend(spectra_here):
    channels_here = spectra_here.shape[1]
    reach = BAND // 2 // channels_here
    below = [shifted(spectra_here, "chan", step_count) for step_count in range(reach, 0, -1)]
    above = [shifted(spectra_here, "chan", -step_count) for step_count in range(1, reach + 1)]
    return jnp.concatenate(below + [spectra_here] + above, axis=1)


def lag_terms(extended, lag_table, channels_here, count):
    half_band = (extended.shape[1] - channels_here) // 2
    group = math.gcd(count, 16)
    own_block = extended[:, half_band : half_band + channels_here].astype(jnp.float32)
    table_rows = lag_table.reshape(2 * lag_table.shape[1], lag_table.shape[2])

    def one_group(index, accumulated):
        first = index * group
        partners = []
        for member in range(group):
            offset = first + member
            position = offset + (offset >= half_band).astype(jnp.int32)
            partners.append(lax.dynamic_slice_in_dim(extended, position, channels_here, 1))
        partner = jnp.stack(partners, axis=0).astype(jnp.float32)
        cross_re = (
            own_block[None, :, :, 0] * partner[:, :, :, 0]
            + own_block[None, :, :, 1] * partner[:, :, :, 1]
        )
        cross_im = (
            own_block[None, :, :, 1] * partner[:, :, :, 0]
            - own_block[None, :, :, 0] * partner[:, :, :, 1]
        )
        joined = jnp.concatenate([cross_re, cross_im], axis=-1).astype(jnp.bfloat16)
        term = jnp.einsum("gwck,kl->gcl", joined, table_rows, preferred_element_type=jnp.float32)
        return lax.dynamic_update_slice_in_dim(accumulated, term, index * group, 0)

    initial = jnp.zeros((count, channels_here, table_rows.shape[-1]), jnp.float32)
    return lax.fori_loop(0, count // group, one_group, initial)


def local(recordings, channel_live):
    windows_here, channels_here, sample_count = recordings.shape
    bin_count = sample_count // 2
    block_width = math.gcd(bin_count, 512)
    samples_flat = recordings.reshape(windows_here * channels_here, sample_count)
    pieces = [
        forward_block(samples_flat, first_bin, block_width, sample_count)
        for first_bin in range(0, bin_count, block_width)
    ]
    spec_re = jnp.concatenate([piece[:, :block_width] for piece in pieces], axis=-1).reshape(
        windows_here, channels_here, bin_count
    )
    spec_im = jnp.concatenate([piece[:, block_width:] for piece in pieces], axis=-1).reshape(
        windows_here, channels_here, bin_count
    )
    whitened = whiten(spec_re, spec_im, channel_live, WB)
    windows = windows_here * lax.axis_size("win")
    lag_table = inverse_table(
        bin_count, sample_count, LAGS, 1.0 / math.sqrt(windows * bin_count)
    ).astype(jnp.bfloat16)
    band_share = BAND // lax.axis_size("win")
    extended = band_extend(whitened)
    return lax.psum_scatter(
        lag_terms(extended, lag_table, channels_here, lax.axis_size("win") * band_share).astype(
            jnp.bfloat16
        ),
        "win",
        scatter_dimension=0,
        tiled=True,
    ).astype(jnp.float32)


def solution(mesh):
    placed = (P("win", "chan", None), P("chan"))
    return jax.shard_map(
        local, mesh=mesh, in_specs=placed, out_specs=P("win", "chan", None), check_vma=False
    )
```

profile of v0, /device:TPU:97, one launch (start us, length us, event | category | flops | bytes accessed | tf_op | source)
XLA Modules:
  0.0 427.3 jit_solution(7740325182157368905)
XLA Ops:
  6.6 35.1 %negate_convert_fusion.3 = (bf16[4096,512]{1,0:T(8,128)(2,1)}, bf16[4096,512]{1,0:T(8,128)(2,1)}) fusion(), kind=kLoop, calls=%fused_computation.80 | loop fusion | flops 35651584 | bytes 8388608 | tf_op jit(solution)/shard_map/convert.15
  41.7 34.0 %cosine_convert_fusion.1 = (bf16[4096,512]{1,0:T(8,128)(2,1)S(1)}, bf16[4096,512]{1,0:T(8,128)(2,1)S(1)}) fusion(s32[512]{0:T(512)S(1)} %iota_add_fusion.1), kind=kLoop, calls=%fused_computation.73 | loop fusion | flops 35651584 | bytes 8390656 | tf_op jit(solution)/shard_map/convert.10
  75.7 34.1 %cosine_convert_fusion = (bf16[4096,512]{1,0:T(8,128)(2,1)S(1)}, bf16[4096,512]{1,0:T(8,128)(2,1)S(1)}) fusion(s32[512]{0:T(512)S(1)} %iota_add_fusion), kind=kLoop, calls=%fused_computation.69 | loop fusion | flops 35651584 | bytes 8390656 | tf_op jit(solution)/shard_map/convert.8
  109.8 1.2 fusion.48
  111.0 1.2 fusion.45
  112.5 34.0 %cosine_convert_fusion.2 = (bf16[4096,512]{1,0:T(8,128)(2,1)S(1)}, bf16[4096,512]{1,0:T(8,128)(2,1)S(1)}) fusion(s32[512]{0:T(512)S(1)} %iota_add_fusion.2), kind=kLoop, calls=%fused_computation.77 | loop fusion | flops 35651584 | bytes 8390656 | tf_op jit(solution)/shard_map/convert.12
  146.5 1.2 fusion.51
  147.9 4.1 fusion.54
  152.6 5.2 %collective-permute-start = (bf16[1,8,2,2048]{3,1,2,0:T(8,128)(2,1)S(1)}, bf16[1,8,2,2048]{3,1,2,0:T(8,128)(2,1)S(1)}, u32[]{:S(2)}, u32[]{:S(2)}) collective-permute-start(bf16[1,8,2,2048]{3,1,2,0:T(8,128)(2,1)S(1)} %pad_maximum_fusion.1), channel_id=1, source_target_pairs={{0,64},{8,72},{16,80},{24,88},{32,96},{40,104},{48,112},{56,120},{... | collective-permute-start | bytes 196616 | tf_op jit(solution)/shard_map/ppermute | solution.py:16
  157.8 3.9 collective-permute-start.1
  161.8 1.9 collective-permute-start.2
  163.7 3.2 collective-permute-start.3
  166.9 1.9 collective-permute-start.4
  168.9 4.5 %multiply_convert_fusion.1 = (bf16[1,2048,128]{2,1,0:T(8,128)(2,1)S(1)}, bf16[1,2048,128]{2,1,0:T(8,128)(2,1)S(1)}) fusion(s32[128]{0:T(128)S(1)} %iota_add_fusion.3), kind=kLoop, calls=%fused_computation.100 | loop fusion | flops 4980736 | bytes 1049088 | tf_op jit(solution)/shard_map/convert.2
  173.5 2.4 collective-permute-start.5
  175.9 2.2 collective-permute-start.6
  178.1 3.1 collective-permute-start.7
  181.2 2.0 collective-permute-start.8
  183.3 4.2 collective-permute-start.9
  187.5 5.1 %collective-permute-start.10 = (bf16[1,8,2,2048]{3,1,2,0:T(8,128)(2,1)S(1)}, bf16[1,8,2,2048]{3,1,2,0:T(8,128)(2,1)S(1)}, u32[]{:S(2)}, u32[]{:S(2)}) collective-permute-start(bf16[1,8,2,2048]{3,1,2,0:T(8,128)(2,1)S(1)} %pad_maximum_fusion.1), channel_id=1, source_target_pairs={{24,0},{32,8},{40,16},{48,24},{56,32},{64,40},{72,48},{80,56},{88,... | collective-permute-start | bytes 196616 | tf_op jit(solution)/shard_map/ppermute | solution.py:16
  192.6 3.4 collective-permute-start.11
  196.0 2.5 collective-permute-start.12
  198.5 2.5 collective-permute-start.13
  201.1 1.9 collective-permute-start.14
  203.1 1.9 collective-permute-start.15
  205.7 4.3 %collective-permute-done.14 = bf16[1,8,2,2048]{3,1,2,0:T(8,128)(2,1)S(1)} collective-permute-done((bf16[1,8,2,2048]{3,1,2,0:T(8,128)(2,1)S(1)}, bf16[1,8,2,2048]{3,1,2,0:T(8,128)(2,1)S(1)}, u32[]{:S(2)}, u32[]{:S(2)}) %collective-permute-start.14) | collective-permute-done | bytes 65568 | tf_op jit(solution)/shard_map/ppermute | solution.py:16
  210.0 3.4 collective-permute-done.15
  213.4 1.0 copy-done.1
  214.4 129.8 %while.13 = (s32[]{:T(128)}, bf16[128,8,128]{2,1,0:T(8,128)(2,1)S(1)}, f32[1,8,2,2048]{3,1,2,0:T(8,128)S(1)}, bf16[1,136,2,2048]{3,1,2,0:T(8,128)(2,1)}, bf16[40...) while((s32[]{:T(128)}, ...), condition=%wide.region_2.3_spmd, body=%wide.region_1.2_spmd.sunk | while | flops 138936432 | bytes 10945987 | solution.py:85
  215.4 0.9 bitcast_dynamic-update-slice_fusion.33
  344.9 74.1 %reduce-scatter.2.cloned.1.call-done = bf16[16,8,128]{2,1,0:T(8,128)(2,1)} async-done(((bf16[128,8,128]{2,1,0:T(8,128)(2,1)}), bf16[16,8,128]{2,1,0:T(8,128)(2,1)}) %reduce-scatter.2.cloned.1.call-update) | async-done | bytes 32784 | tf_op jit(solution)/shard_map/reduce_scatter | solution.py:110
  419.0 1.4 convert_element_type.225
  (223 shorter events, 129.4 us)
Async XLA Ops:
  6.5 103.2 %copy-start = (bf16[1,8,4096]{2,1,0:T(8,128)(2,1)S(1)}, bf16[1,8,4096]{2,1,0:T(8,128)(2,1)}, u32[]{:S(2)}) copy-start(bf16[1,8,4096]{2,1,0:T(8,128)(2,1)} %param.4) | copy-start | bytes 196612
  6.5 412.5 %reduce-scatter.2.cloned.1.call-start = ((), (), s32[]{:S(2)}) async-start(), calls=%async_computation.1 | async-start | bytes 294912 | tf_op jit(solution)/shard_map/reduce_scatter | solution.py:110
  147.9 4.6 %copy-start.3 = (s32[8]{0:T(128)S(1)}, s32[8]{0:T(128)}, u32[]{:S(2)}) copy-start(s32[8]{0:T(128)} %param.5) | copy-start | bytes 100
  152.6 20.8 %collective-permute-start = (bf16[1,8,2,2048]{3,1,2,0:T(8,128)(2,1)S(1)}, bf16[1,8,2,2048]{3,1,2,0:T(8,128)(2,1)S(1)}, u32[]{:S(2)}, u32[]{:S(2)}) collective-permute-start(bf16[1,8,2,2048]{3,1,2,0:T(8,128)(2,1)S(1)} %pad_maximum_fusion.1), channel_id=1, source_target_pairs={{0,64},{8,72},{16,80},{24,88},{32,96},{40,104},{48,112},{56,120},{... | collective-permute-start | bytes 196616 | tf_op jit(solution)/shard_map/ppermute | solution.py:16
  157.8 18.0 %collective-permute-start.1 = (bf16[1,8,2,2048]{3,1,2,0:T(8,128)(2,1)S(1)}, bf16[1,8,2,2048]{3,1,2,0:T(8,128)(2,1)S(1)}, u32[]{:S(2)}, u32[]{:S(2)}) collective-permute-start(bf16[1,8,2,2048]{3,1,2,0:T(8,128)(2,1)S(1)} %pad_maximum_fusion.1), channel_id=1, source_target_pairs={{0,56},{8,64},{16,72},{24,80},{32,88},{40,96},{48,104},{56,112},{6... | collective-permute-start | bytes 196616 | tf_op jit(solution)/shard_map/ppermute | solution.py:16
  161.8 16.3 %collective-permute-start.2 = (bf16[1,8,2,2048]{3,1,2,0:T(8,128)(2,1)S(1)}, bf16[1,8,2,2048]{3,1,2,0:T(8,128)(2,1)S(1)}, u32[]{:S(2)}, u32[]{:S(2)}) collective-permute-start(bf16[1,8,2,2048]{3,1,2,0:T(8,128)(2,1)S(1)} %pad_maximum_fusion.1), channel_id=1, source_target_pairs={{0,48},{8,56},{16,64},{24,72},{32,80},{40,88},{48,96},{56,104},{64... | collective-permute-start | bytes 196616 | tf_op jit(solution)/shard_map/ppermute | solution.py:16
  163.7 17.5 %collective-permute-start.3 = (bf16[1,8,2,2048]{3,1,2,0:T(8,128)(2,1)S(1)}, bf16[1,8,2,2048]{3,1,2,0:T(8,128)(2,1)S(1)}, u32[]{:S(2)}, u32[]{:S(2)}) collective-permute-start(bf16[1,8,2,2048]{3,1,2,0:T(8,128)(2,1)S(1)} %pad_maximum_fusion.1), channel_id=1, source_target_pairs={{0,40},{8,48},{16,56},{24,64},{32,72},{40,80},{48,88},{56,96},{64,... | collective-permute-start | bytes 196616 | tf_op jit(solution)/shard_map/ppermute | solution.py:16
  166.9 16.4 %collective-permute-start.4 = (bf16[1,8,2,2048]{3,1,2,0:T(8,128)(2,1)S(1)}, bf16[1,8,2,2048]{3,1,2,0:T(8,128)(2,1)S(1)}, u32[]{:S(2)}, u32[]{:S(2)}) collective-permute-start(bf16[1,8,2,2048]{3,1,2,0:T(8,128)(2,1)S(1)} %pad_maximum_fusion.1), channel_id=1, source_target_pairs={{0,32},{8,40},{16,48},{24,56},{32,64},{40,72},{48,80},{56,88},{64,... | collective-permute-start | bytes 196616 | tf_op jit(solution)/shard_map/ppermute | solution.py:16
  173.5 14.0 %collective-permute-start.5 = (bf16[1,8,2,2048]{3,1,2,0:T(8,128)(2,1)S(1)}, bf16[1,8,2,2048]{3,1,2,0:T(8,128)(2,1)S(1)}, u32[]{:S(2)}, u32[]{:S(2)}) collective-permute-start(bf16[1,8,2,2048]{3,1,2,0:T(8,128)(2,1)S(1)} %pad_maximum_fusion.1), channel_id=1, source_target_pairs={{0,24},{8,32},{16,40},{24,48},{32,56},{40,64},{48,72},{56,80},{64,... | collective-permute-start | bytes 196616 | tf_op jit(solution)/shard_map/ppermute | solution.py:16
  175.9 16.7 %collective-permute-start.6 = (bf16[1,8,2,2048]{3,1,2,0:T(8,128)(2,1)S(1)}, bf16[1,8,2,2048]{3,1,2,0:T(8,128)(2,1)S(1)}, u32[]{:S(2)}, u32[]{:S(2)}) collective-permute-start(bf16[1,8,2,2048]{3,1,2,0:T(8,128)(2,1)S(1)} %pad_maximum_fusion.1), channel_id=1, source_target_pairs={{0,16},{8,24},{16,32},{24,40},{32,48},{40,56},{48,64},{56,72},{64,... | collective-permute-start | bytes 196616 | tf_op jit(solution)/shard_map/ppermute | solution.py:16
  178.1 17.9 %collective-permute-start.7 = (bf16[1,8,2,2048]{3,1,2,0:T(8,128)(2,1)S(1)}, bf16[1,8,2,2048]{3,1,2,0:T(8,128)(2,1)S(1)}, u32[]{:S(2)}, u32[]{:S(2)}) collective-permute-start(bf16[1,8,2,2048]{3,1,2,0:T(8,128)(2,1)S(1)} %pad_maximum_fusion.1), channel_id=1, source_target_pairs={{0,8},{8,16},{16,24},{24,32},{32,40},{40,48},{48,56},{56,64},{64,7... | collective-permute-start | bytes 196616 | tf_op jit(solution)/shard_map/ppermute | solution.py:16
  181.2 17.3 %collective-permute-start.8 = (bf16[1,8,2,2048]{3,1,2,0:T(8,128)(2,1)S(1)}, bf16[1,8,2,2048]{3,1,2,0:T(8,128)(2,1)S(1)}, u32[]{:S(2)}, u32[]{:S(2)}) collective-permute-start(bf16[1,8,2,2048]{3,1,2,0:T(8,128)(2,1)S(1)} %pad_maximum_fusion.1), channel_id=1, source_target_pairs={{8,0},{16,8},{24,16},{32,24},{40,32},{48,40},{56,48},{64,56},{72,6... | collective-permute-start | bytes 196616 | tf_op jit(solution)/shard_map/ppermute | solution.py:16
  183.3 17.8 %collective-permute-start.9 = (bf16[1,8,2,2048]{3,1,2,0:T(8,128)(2,1)S(1)}, bf16[1,8,2,2048]{3,1,2,0:T(8,128)(2,1)S(1)}, u32[]{:S(2)}, u32[]{:S(2)}) collective-permute-start(bf16[1,8,2,2048]{3,1,2,0:T(8,128)(2,1)S(1)} %pad_maximum_fusion.1), channel_id=1, source_target_pairs={{16,0},{24,8},{32,16},{40,24},{48,32},{56,40},{64,48},{72,56},{80,... | collective-permute-start | bytes 196616 | tf_op jit(solution)/shard_map/ppermute | solution.py:16
  187.5 15.6 %collective-permute-start.10 = (bf16[1,8,2,2048]{3,1,2,0:T(8,128)(2,1)S(1)}, bf16[1,8,2,2048]{3,1,2,0:T(8,128)(2,1)S(1)}, u32[]{:S(2)}, u32[]{:S(2)}) collective-permute-start(bf16[1,8,2,2048]{3,1,2,0:T(8,128)(2,1)S(1)} %pad_maximum_fusion.1), channel_id=1, source_target_pairs={{24,0},{32,8},{40,16},{48,24},{56,32},{64,40},{72,48},{80,56},{88,... | collective-permute-start | bytes 196616 | tf_op jit(solution)/shard_map/ppermute | solution.py:16
  192.6 12.4 %collective-permute-start.11 = (bf16[1,8,2,2048]{3,1,2,0:T(8,128)(2,1)S(1)}, bf16[1,8,2,2048]{3,1,2,0:T(8,128)(2,1)S(1)}, u32[]{:S(2)}, u32[]{:S(2)}) collective-permute-start(bf16[1,8,2,2048]{3,1,2,0:T(8,128)(2,1)S(1)} %pad_maximum_fusion.1), channel_id=1, source_target_pairs={{32,0},{40,8},{48,16},{56,24},{64,32},{72,40},{80,48},{88,56},{96,... | collective-permute-start | bytes 196616 | tf_op jit(solution)/shard_map/ppermute | solution.py:16
  196.0 9.0 %collective-permute-start.12 = (bf16[1,8,2,2048]{3,1,2,0:T(8,128)(2,1)S(1)}, bf16[1,8,2,2048]{3,1,2,0:T(8,128)(2,1)S(1)}, u32[]{:S(2)}, u32[]{:S(2)}) collective-permute-start(bf16[1,8,2,2048]{3,1,2,0:T(8,128)(2,1)S(1)} %pad_maximum_fusion.1), channel_id=1, source_target_pairs={{40,0},{48,8},{56,16},{64,24},{72,32},{80,40},{88,48},{96,56},{104... | collective-permute-start | bytes 196616 | tf_op jit(solution)/shard_map/ppermute | solution.py:16
  198.5 7.1 %collective-permute-start.13 = (bf16[1,8,2,2048]{3,1,2,0:T(8,128)(2,1)S(1)}, bf16[1,8,2,2048]{3,1,2,0:T(8,128)(2,1)S(1)}, u32[]{:S(2)}, u32[]{:S(2)}) collective-permute-start(bf16[1,8,2,2048]{3,1,2,0:T(8,128)(2,1)S(1)} %pad_maximum_fusion.1), channel_id=1, source_target_pairs={{48,0},{56,8},{64,16},{72,24},{80,32},{88,40},{96,48},{104,56},{11... | collective-permute-start | bytes 196616 | tf_op jit(solution)/shard_map/ppermute | solution.py:16
  201.1 8.8 %collective-permute-start.14 = (bf16[1,8,2,2048]{3,1,2,0:T(8,128)(2,1)S(1)}, bf16[1,8,2,2048]{3,1,2,0:T(8,128)(2,1)S(1)}, u32[]{:S(2)}, u32[]{:S(2)}) collective-permute-start(bf16[1,8,2,2048]{3,1,2,0:T(8,128)(2,1)S(1)} %pad_maximum_fusion.1), channel_id=1, source_target_pairs={{56,0},{64,8},{72,16},{80,24},{88,32},{96,40},{104,48},{112,56},{1... | collective-permute-start | bytes 196616 | tf_op jit(solution)/shard_map/ppermute | solution.py:16
  203.1 10.3 %collective-permute-start.15 = (bf16[1,8,2,2048]{3,1,2,0:T(8,128)(2,1)S(1)}, bf16[1,8,2,2048]{3,1,2,0:T(8,128)(2,1)S(1)}, u32[]{:S(2)}, u32[]{:S(2)}) collective-permute-start(bf16[1,8,2,2048]{3,1,2,0:T(8,128)(2,1)S(1)} %pad_maximum_fusion.1), channel_id=1, source_target_pairs={{64,0},{72,8},{80,16},{88,24},{96,32},{104,40},{112,48},{120,56},{... | collective-permute-start | bytes 196616 | tf_op jit(solution)/shard_map/ppermute | solution.py:16
  213.4 1.0 copy-start.1
  344.2 0.7 copy-start.2
Sparse Core Ops, SparseCore 0:
  345.1 73.9 reduce-scatter.1
where the time goes:
time: 433 us; the launch traced here: 427 us
  other arithmetic  147 us (34%)
  local copies, waits for them, and re-layouts  123 us (28%)
  waiting for transfers between devices  82.5 us (19%)
  starting transfers between devices  47.4 us (11%)
  between operations  13.9 us (3%)
  matrix products  11.3 us (3%)
    another operation x13, other arithmetic  144 us
    while x120, local copies, waits for them, and re-layouts  113 us
    reduce_scatter x1, waiting for transfers between devices, local(): lax.psum_scatter(lag_terms(extended, lag_table, channels_here, lax.axis_s...  74.1 us
    ppermute x16, starting transfers between devices, shifted(): lax.ppermute(value, axis, [(source, source + steps) for source in range(l...  47.4 us
  transfers between devices with their start and end apart: 17, of which 4 were waited for; matrix products, arithmetic and copies ran while one was open for 1% of the time, Pallas kernels for 0%

commit v1 on v0

v1 whole, which is shorter than its diff:
```python
import math

import jax
import jax.numpy as jnp
import numpy as np
from jax import lax
from jax.experimental import pallas as pl
from jax.experimental.pallas import tpu as pltpu
from jax.sharding import PartitionSpec as P

NT = 4096
NF = 2048
WB = 64
BAND = 128
LAGS = 128
C = 8
N1 = 16
N2 = 256
K1 = 16
K2 = 128
REACH = BAND // 2 // C
SLOTS = 2 * REACH + 1
MESH = pl.DeviceIdType.MESH


def bin_order():
    lane = np.arange(K2)
    return 4 * (lane % 32) + lane // 32


def tables(window_count):
    tau = 2.0 * math.pi
    k1, n1, n2 = np.arange(K1), np.arange(N1), np.arange(N2)
    k2 = bin_order()
    first = tau * (np.outer(k1, n1) % 16) / 16.0
    first = np.concatenate([np.cos(first), -np.sin(first)], axis=0)
    first = np.kron(first, np.eye(C))
    twiddle = tau * (np.outer(k1, n2) % NT) / NT
    twiddle = np.stack([np.cos(twiddle), -np.sin(twiddle)])
    twiddle = np.repeat(twiddle, C, axis=1)
    second = tau * (np.outer(n2, k2) % N2) / N2
    cos, sin = np.cos(second), np.sin(second)
    second = np.block([[cos, -sin], [sin, cos]])
    bins = k1[:, None] + K1 * k2[None, :]
    lag = tau * ((bins[:, :, None] * (np.arange(LAGS) - LAGS // 2)) % NT) / NT
    factor = 1.0 / math.sqrt(window_count * NF)
    lag = np.concatenate([np.cos(lag) * factor, -np.sin(lag) * factor], axis=1)
    return (
        jnp.asarray(first, jnp.bfloat16),
        jnp.asarray(twiddle, jnp.float32),
        jnp.asarray(second, jnp.bfloat16),
        jnp.asarray(lag, jnp.bfloat16),
    )


def kernel(
    chans,
    wins,
    live_ref,
    x_ref,
    first_ref,
    twiddle_ref,
    second_ref,
    lag_ref,
    out_ref,
    halo,
    ownb,
    acc,
    sums_out,
    sums_in,
    halo_send,
    halo_recv,
    sums_send,
    sums_recv,
):
    j = lax.axis_index("chan")
    w = lax.axis_index("win")
    group = BAND // wins

    barrier = pltpu.get_barrier_semaphore()
    for d in range(1, REACH + 1):
        for there in (j - d, j + d):

            @pl.when((there >= 0) & (there < chans))
            def _():
                pl.semaphore_signal(
                    barrier, inc=1, device_id={"chan": there}, device_id_type=MESH
                )

    for d in range(1, wins):
        pl.semaphore_signal(
            barrier, inc=1, device_id={"win": lax.rem(w + d, wins)}, device_id_type=MESH
        )

    x = x_ref[0].astype(jnp.float32)
    pieces = jnp.concatenate([x[:, N2 * n1 : N2 * (n1 + 1)] for n1 in range(N1)], axis=0)
    s = jnp.dot(first_ref[...], pieces.astype(jnp.bfloat16), preferred_element_type=jnp.float32)
    s_re, s_im = s[: K1 * C], s[K1 * C :]
    t_re, t_im = twiddle_ref[0], twiddle_ref[1]
    y = jnp.concatenate([s_re * t_re - s_im * t_im, s_re * t_im + s_im * t_re], axis=1)
    spec = jnp.dot(y.astype(jnp.bfloat16), second_ref[...], preferred_element_type=jnp.float32)
    energy = spec[:, :K2] * spec[:, :K2] + spec[:, K2:] * spec[:, K2:]
    energy = jnp.sum(energy.reshape(K1, C, K2), axis=0)
    energy = energy + pltpu.roll(energy, 64, 1)
    energy = energy + pltpu.roll(energy, 32, 1)
    row = lax.broadcasted_iota(jnp.int32, (C, K2), 0)
    live = jnp.zeros((C, K2), jnp.float32)
    for c in range(C):
        live = jnp.where(row == c, live_ref[c].astype(jnp.float32), live)
    factor = (1.0 / jnp.sqrt(energy * (1.0 / WB) + 1e-6)) * live
    factor = jnp.broadcast_to(factor[None], (K1, C, K2)).reshape(K1 * C, K2)
    white_re = (spec[:, :K2] * factor).astype(jnp.bfloat16)
    white_im = (spec[:, K2:] * factor).astype(jnp.bfloat16)
    halo[REACH, 0] = white_re
    halo[REACH, 1] = white_im

    present = jnp.minimum(j, REACH) + jnp.minimum(chans - 1 - j, REACH)
    pl.semaphore_wait(barrier, present + (wins - 1))

    def halo_copy(slot, there):
        return pltpu.make_async_remote_copy(
            src_ref=halo.at[REACH],
            dst_ref=halo.at[slot],
            send_sem=halo_send.at[slot],
            recv_sem=halo_recv.at[slot],
            device_id={"chan": there},
            device_id_type=MESH,
        )

    for d in range(1, REACH + 1):
        for sign in (-1, 1):
            there = j + sign * d
            slot = REACH - sign * d

            @pl.when((there >= 0) & (there < chans))
            def _():
                halo_copy(slot, there).start()

            @pl.when((j - sign * d < 0) | (j - sign * d >= chans))
            def _():
                halo[slot] = jnp.zeros((2, K1 * C, K2), jnp.bfloat16)

    ownb[0] = jnp.broadcast_to(
        white_re.astype(jnp.float32)[:, None, :], (K1 * C, 8, K2)
    )
    ownb[1] = jnp.broadcast_to(
        white_im.astype(jnp.float32)[:, None, :], (K1 * C, 8, K2)
    )

    def cross_terms(slots):
        total = jnp.zeros((64 * len(slots), LAGS), jnp.float32)
        for pair in range(K1 // 2):
            rows = slice(16 * pair, 16 * pair + 16)
            blocks = [
                (
                    halo[slot, 0, rows].astype(jnp.float32),
                    halo[slot, 1, rows].astype(jnp.float32),
                )
                for slot in slots
            ]
            for half in (0, 1):
                k1 = 2 * pair + half
                own_re, own_im = ownb[0, C * k1 : C * k1 + C], ownb[1, C * k1 : C * k1 + C]
                parts = []
                for block_re, block_im in blocks:
                    p_re = block_re[8 * half : 8 * half + 8][None]
                    p_im = block_im[8 * half : 8 * half + 8][None]
                    re = own_re * p_re + own_im * p_im
                    im = own_im * p_re - own_re * p_im
                    parts.append(
                        jnp.concatenate([re.reshape(64, K2), im.reshape(64, K2)], axis=1)
                    )
                cross = jnp.concatenate(parts, axis=0).astype(jnp.bfloat16)
                total += jnp.dot(cross, lag_ref[k1], preferred_element_type=jnp.float32)
        for index, slot in enumerate(slots):
            for c in range(C):
                value = total[64 * index + 8 * c : 64 * index + 8 * c + 8]
                acc[pl.ds(8 * slot + 7 - c, 8), c, :] = value

    def group_start(g):
        return group * g + 7 + (g >= wins // 2).astype(jnp.int32)

    def sums_copy(g):
        return pltpu.make_async_remote_copy(
            src_ref=sums_out.at[g],
            dst_ref=sums_in.at[w],
            send_sem=sums_send.at[g],
            recv_sem=sums_recv.at[w],
            device_id={"win": g},
            device_id_type=MESH,
        )

    cross_terms([REACH])

    def step(index, _):
        for d in (2 * index + 1, 2 * index + 2):
            for sign in (-1, 1):

                @pl.when((j + sign * d >= 0) & (j + sign * d < chans))
                def _():
                    halo_copy(REACH + sign * d, j).wait_recv()

            cross_terms([REACH - d, REACH + d])
        for g in (wins // 2 - 1 - index, wins // 2 + index):

            @pl.when(g != w)
            def _():
                value = acc[pl.ds(group_start(g), group)]
                sums_out[g] = value.reshape(group * C, LAGS).astype(jnp.bfloat16)
                sums_copy(g).start()

        return 0

    lax.fori_loop(0, wins // 2, step, 0)

    out_ref[...] = acc[pl.ds(group_start(w), group)]

    def gather(step, _):
        source = lax.rem(w + step, wins)
        pltpu.make_async_remote_copy(
            src_ref=sums_out.at[source],
            dst_ref=sums_in.at[source],
            send_sem=sums_send.at[source],
            recv_sem=sums_recv.at[source],
            device_id={"win": source},
            device_id_type=MESH,
        ).wait_recv()
        out_ref[...] += sums_in[source].astype(jnp.float32).reshape(group, C, LAGS)
        return 0

    lax.fori_loop(1, wins, gather, 0)

    for g in range(wins):

        @pl.when(g != w)
        def _():
            sums_copy(g).wait_send()

    for d in range(1, REACH + 1):
        for sign in (-1, 1):

            @pl.when((j + sign * d >= 0) & (j + sign * d < chans))
            def _():
                halo_copy(REACH - sign * d, j + sign * d).wait_send()


def solution(mesh):
    chans, wins = mesh.shape["chan"], mesh.shape["win"]
    group = BAND // wins

    def local(recordings, channel_live):
        first, twiddle, second, lag = tables(wins * recordings.shape[0])
        vmem = pl.BlockSpec(memory_space=pltpu.VMEM)

        def body(*refs):
            kernel(chans, wins, *refs)

        return pl.pallas_call(
            body,
            out_shape=jax.ShapeDtypeStruct((group, C, LAGS), jnp.float32),
            in_specs=[pl.BlockSpec(memory_space=pltpu.SMEM)] + [vmem] * 5,
            out_specs=vmem,
            scratch_shapes=[
                pltpu.VMEM((SLOTS, 2, K1 * C, K2), jnp.bfloat16),
                pltpu.VMEM((2, K1 * C, 8, K2), jnp.float32),
                pltpu.VMEM((8 * SLOTS + 7, C, LAGS), jnp.float32),
                pltpu.VMEM((wins, group * C, LAGS), jnp.bfloat16),
                pltpu.VMEM((wins, group * C, LAGS), jnp.bfloat16),
                pltpu.SemaphoreType.DMA((SLOTS,)),
                pltpu.SemaphoreType.DMA((SLOTS,)),
                pltpu.SemaphoreType.DMA((wins,)),
                pltpu.SemaphoreType.DMA((wins,)),
            ],
            compiler_params=pltpu.CompilerParams(
                collective_id=0, has_side_effects=True, vmem_limit_bytes=24 * 1024 * 1024
            ),
            name="correlate",
        )(channel_live, recordings, first, twiddle, second, lag)

    return jax.shard_map(
        local,
        mesh=mesh,
        in_specs=(P("win", "chan", None), P("chan")),
        out_specs=P("win", "chan", None),
        check_vma=False,
    )
```

time: 433 us -> 40.8 us (0.09)
  the two profiles are of different devices: /device:TPU:97 before, /device:TPU:32 now
where the time goes in v1:
time: 40.8 us; the launch traced here: 40.5 us
  Pallas kernels  34.4 us (84%)
  local copies, waits for them, and re-layouts  6.09 us (15%)
    pallas_call x1, Pallas kernels, local(): pl.pallas_call(body, out_shape=jax.ShapeDtypeStruct((group, C, LAGS), jnp...  34.4 us
    unnamed x13, local copies, waits for them, and re-layouts  6.09 us

profile of v1, /device:TPU:32, one launch (start us, length us, event | category | flops | bytes accessed | tf_op | source)
XLA Modules:
  0.0 40.5 jit_solution(1375466123110246210)
XLA Ops:
  0.0 0.0 copy-start
  0.0 1.2 %copy-done = bf16[16,256,128]{2,1,0:T(8,128)(2,1)S(1)} copy-done((bf16[16,256,128]{2,1,0:T(8,128)(2,1)S(1)}, bf16[16,256,128]{2,1,0:T(8,128)(2,1)}, u32[]{:S(2)}) %copy-start) | copy-done | bytes 1048600
  1.2 0.0 copy-start.1
  1.2 0.9 %copy-done.1 = bf16[512,256]{1,0:T(8,128)(2,1)S(1)} copy-done((bf16[512,256]{1,0:T(8,128)(2,1)S(1)}, bf16[512,256]{1,0:T(8,128)(2,1)}, u32[]{:S(2)}) %copy-start.1) | copy-done | bytes 262168
  2.2 0.0 copy-start.2
  2.2 0.9 %copy-done.2 = f32[2,128,256]{2,1,0:T(8,128)S(1)} copy-done((f32[2,128,256]{2,1,0:T(8,128)S(1)}, f32[2,128,256]{2,1,0:T(8,128)}, u32[]{:S(2)}) %copy-start.2) | copy-done | bytes 262168
  3.1 0.0 copy-start.3
  3.1 0.8 %copy-done.3 = bf16[1,8,4096]{2,1,0:T(8,128)(2,1)S(1)} copy-done((bf16[1,8,4096]{2,1,0:T(8,128)(2,1)S(1)}, bf16[1,8,4096]{2,1,0:T(8,128)(2,1)}, u32[]{:S(2)}) %copy-start.3) | copy-done | bytes 65560
  4.0 0.0 copy-start.4
  4.0 0.8 %copy-done.4 = bf16[256,128]{1,0:T(8,128)(2,1)S(1)} copy-done((bf16[256,128]{1,0:T(8,128)(2,1)S(1)}, bf16[256,128]{1,0:T(8,128)(2,1)}, u32[]{:S(2)}) %copy-start.4) | copy-done | bytes 65560
  4.8 0.0 copy-start.5
  4.8 0.7 %copy-done.5 = s32[8]{0:T(128)S(1)} copy-done((s32[8]{0:T(128)S(1)}, s32[8]{0:T(128)}, u32[]{:S(2)}) %copy-start.5) | copy-done | bytes 56
  5.5 34.4 %correlate.1 = f32[16,8,128]{2,1,0:T(8,128)S(1)} custom-call(s32[8]{0:T(128)S(1)} %copy-done.5, bf16[1,8,4096]{2,1,0:T(8,128)(2,1)S(1)} %copy-done.3, bf16[256,128]{1,0:T(8,128)(2,1)S(1)} %copy-done.4, f32[2,128,256]{2,1,0:T(8,128)S(1)} %copy-done.2, bf16[512,256]{1,0:T(8,128)(2,1)S(1)} %copy-done.1, bf16[16,256,128]{2,1,0:T(8,128)(2,1)S(1)} %copy-done), custom_call_target="tpu_custom_call" | custom-call | tf_op jit(solution)/shard_map/correlate/pallas_call | solution.py:258
  39.9 0.6 %copy.8 = f32[16,8,128]{2,1,0:T(8,128)} copy(f32[16,8,128]{2,1,0:T(8,128)S(1)} %correlate.1) | data formatting | bytes 131072
Async XLA Ops:
  0.0 1.2 %copy-start = (bf16[16,256,128]{2,1,0:T(8,128)(2,1)S(1)}, bf16[16,256,128]{2,1,0:T(8,128)(2,1)}, u32[]{:S(2)}) copy-start(bf16[16,256,128]{2,1,0:T(8,128)(2,1)} %constant.11.clone.refs_5_) | copy-start | bytes 3145732
  1.2 0.9 %copy-start.1 = (bf16[512,256]{1,0:T(8,128)(2,1)S(1)}, bf16[512,256]{1,0:T(8,128)(2,1)}, u32[]{:S(2)}) copy-start(bf16[512,256]{1,0:T(8,128)(2,1)} %constant.10.clone.refs_4_) | copy-start | bytes 786436
  2.2 0.9 %copy-start.2 = (f32[2,128,256]{2,1,0:T(8,128)S(1)}, f32[2,128,256]{2,1,0:T(8,128)}, u32[]{:S(2)}) copy-start(f32[2,128,256]{2,1,0:T(8,128)} %constant.9.clone.refs_3_) | copy-start | bytes 786436
  3.1 0.8 %copy-start.3 = (bf16[1,8,4096]{2,1,0:T(8,128)(2,1)S(1)}, bf16[1,8,4096]{2,1,0:T(8,128)(2,1)}, u32[]{:S(2)}) copy-start(bf16[1,8,4096]{2,1,0:T(8,128)(2,1)} %refs_1_.1) | copy-start | bytes 196612
  4.0 0.8 %copy-start.4 = (bf16[256,128]{1,0:T(8,128)(2,1)S(1)}, bf16[256,128]{1,0:T(8,128)(2,1)}, u32[]{:S(2)}) copy-start(bf16[256,128]{1,0:T(8,128)(2,1)} %constant.8.clone.refs_2_) | copy-start | bytes 196612
  4.8 0.7 %copy-start.5 = (s32[8]{0:T(128)S(1)}, s32[8]{0:T(128)}, u32[]{:S(2)}) copy-start(s32[8]{0:T(128)} %refs_0_.1) | copy-start | bytes 100

commit v2 on v1

v2 whole, which is shorter than its diff:
```python
import math

import jax
import jax.numpy as jnp
import numpy as np
from jax import lax
from jax.experimental import pallas as pl
from jax.experimental.pallas import tpu as pltpu
from jax.sharding import PartitionSpec as P

NT = 4096
NF = 2048
WB = 64
BAND = 128
LAGS = 128
C = 8
N1 = 16
N2 = 256
K1 = 16
K2 = 128
PLANE = 4
PLANES = 5
SLOTS = PLANE * PLANES
UP, DOWN, SIDE, CORE = range(4)
MESH = pl.DeviceIdType.MESH


def bin_order():
    lane = np.arange(K2)
    return 4 * (lane % 32) + lane // 32


def tables(window_count):
    tau = 2.0 * math.pi
    k1, n1, n2 = np.arange(K1), np.arange(N1), np.arange(N2)
    k2 = bin_order()
    first = tau * (np.outer(k1, n1) % 16) / 16.0
    first = np.concatenate([np.cos(first), -np.sin(first)], axis=0)
    first = np.kron(first, np.eye(C))
    twiddle = tau * (np.outer(k1, n2) % NT) / NT
    twiddle = np.stack([np.cos(twiddle), -np.sin(twiddle)])
    twiddle = np.repeat(twiddle, C, axis=1)
    second = tau * (np.outer(n2, k2) % N2) / N2
    cos, sin = np.cos(second), np.sin(second)
    second = np.stack([np.concatenate([cos, sin]), np.concatenate([-sin, cos])])
    bins = k1[:, None] + K1 * k2[None, :]
    lag = tau * ((bins[:, :, None] * (np.arange(LAGS) - LAGS // 2)) % NT) / NT
    factor = 1.0 / math.sqrt(window_count * NF)
    lag = np.concatenate([np.cos(lag) * factor, -np.sin(lag) * factor], axis=1)
    return (
        jnp.asarray(first, jnp.bfloat16),
        jnp.asarray(twiddle, jnp.float32),
        jnp.asarray(second, jnp.bfloat16),
        jnp.asarray(lag, jnp.bfloat16),
    )


def kernel(
    chans,
    wins,
    live_hbm,
    x_hbm,
    first_hbm,
    twiddle_hbm,
    second_hbm,
    lag_hbm,
    out_ref,
    live_ref,
    x_ref,
    first_ref,
    twiddle_ref,
    second_ref,
    lag_ref,
    halo,
    ownb,
    acc,
    sums_out,
    sums_in,
    fetch_sem,
    halo_send,
    halo_recv,
    sums_send,
    sums_recv,
):
    j = lax.axis_index("chan")
    w = lax.axis_index("win")
    group = BAND // wins
    planes = chans // PLANE
    z, r = j // PLANE, j % PLANE
    y, core = r // 2, r % 2
    other = 1 - core
    column, beside = 2 * y, 2 - 2 * y
    own = 2 * PLANE + r

    fetches = [
        pltpu.make_async_copy(source, target, fetch_sem.at[index])
        for index, (source, target) in enumerate(
            (
                (x_hbm, x_ref),
                (first_hbm, first_ref),
                (twiddle_hbm, twiddle_ref),
                (second_hbm, second_ref),
                (live_hbm, live_ref),
                (lag_hbm, lag_ref),
            )
        )
    ]
    for fetch in fetches:
        fetch.start()

    def exists(plane):
        there = z + plane - 2
        return (there >= 0) & (there < planes)

    neighbours = {
        UP: (j + PLANE, -PLANE),
        DOWN: (j - PLANE, PLANE),
        SIDE: (j + 2 - 4 * y, 0),
        CORE: (j + 1 - 2 * core, 0),
    }

    barrier = pltpu.get_barrier_semaphore()

    def greet(there):
        pl.semaphore_signal(barrier, inc=1, device_id=there, device_id_type=MESH)

    pl.when(exists(3))(lambda: greet({"chan": j + PLANE}))
    pl.when(exists(1))(lambda: greet({"chan": j - PLANE}))
    greet({"chan": neighbours[SIDE][0]})
    greet({"chan": neighbours[CORE][0]})
    for d in range(1, wins):
        greet({"win": lax.rem(w + d, wins)})

    fetches[0].wait()
    fetches[1].wait()
    x = x_ref[0].astype(jnp.float32)
    pieces = jnp.concatenate([x[:, N2 * n1 : N2 * (n1 + 1)] for n1 in range(N1)], axis=0)
    s = jnp.dot(first_ref[...], pieces.astype(jnp.bfloat16), preferred_element_type=jnp.float32)
    s_re, s_im = s[: K1 * C], s[K1 * C :]
    fetches[2].wait()
    fetches[3].wait()
    t_re, t_im = twiddle_ref[0], twiddle_ref[1]
    y_re = (s_re * t_re - s_im * t_im).astype(jnp.bfloat16)
    y_im = (s_re * t_im + s_im * t_re).astype(jnp.bfloat16)
    spec = jnp.dot(
        jnp.concatenate([y_re, y_im], axis=1),
        jnp.concatenate([second_ref[0], second_ref[1]], axis=1),
        preferred_element_type=jnp.float32,
    )
    energy = spec[:, :K2] * spec[:, :K2] + spec[:, K2:] * spec[:, K2:]
    energy = jnp.sum(energy.reshape(K1, C, K2), axis=0)
    energy = energy + pltpu.roll(energy, 64, 1)
    energy = energy + pltpu.roll(energy, 32, 1)
    row = lax.broadcasted_iota(jnp.int32, (C, K2), 0)
    live = jnp.zeros((C, K2), jnp.float32)
    fetches[4].wait()
    for c in range(C):
        live = jnp.where(row == c, live_ref[c].astype(jnp.float32), live)
    factor = (1.0 / jnp.sqrt(energy * (1.0 / WB) + 1e-6)) * live
    factor = jnp.broadcast_to(factor[None], (K1, C, K2)).reshape(K1 * C, K2)
    white_re = (spec[:, :K2] * factor).astype(jnp.bfloat16)
    white_im = (spec[:, K2:] * factor).astype(jnp.bfloat16)
    halo[own, 0] = white_re
    halo[own, 1] = white_im

    beyond = exists(1).astype(jnp.int32) + exists(3).astype(jnp.int32)
    pl.semaphore_wait(barrier, beyond + 2 + (wins - 1))

    def halo_copy(way, slot):
        there, shift = neighbours[way]
        return pltpu.make_async_remote_copy(
            src_ref=halo.at[slot],
            dst_ref=halo.at[slot + shift],
            send_sem=halo_send.at[way, slot],
            recv_sem=halo_recv.at[slot + shift],
            device_id={"chan": there},
            device_id_type=MESH,
        )

    always = j >= 0
    has = [exists(plane) for plane in range(PLANES)]
    inside = has[1] & has[3]
    same, across = column + core, beside + core
    slot_of = [[PLANE * plane + rank for rank in (same, column + other, across, beside + other)] for plane in range(PLANES)]
    SAME, MATE, ACROSS, ACROSS_MATE = range(4)
    plan = {
        (UP, 2, SAME): has[3],
        (DOWN, 2, SAME): has[1],
        (SIDE, 2, SAME): always,
        (CORE, 2, SAME): always,
        (UP, 2, ACROSS): has[3],
        (DOWN, 2, ACROSS): has[1],
        (CORE, 2, ACROSS): always,
        (UP, 1, SAME): inside,
        (CORE, 1, SAME): has[1],
        (DOWN, 3, SAME): inside,
        (CORE, 3, SAME): has[3],
        (UP, 1, ACROSS): inside & (y == 0),
        (CORE, 1, ACROSS): has[1],
        (DOWN, 3, ACROSS): inside & (y == 1),
        (CORE, 3, ACROSS): has[3],
        (CORE, 0, SAME): has[0] & (core == 1),
        (CORE, 4, SAME): has[4] & (core == 0),
        (CORE, 0, ACROSS): has[0] & (y == 0),
        (CORE, 4, ACROSS): has[4] & (y == 1),
    }
    arrivals = {(plane, rank): has[plane] for plane in (1, 3) for rank in range(4)}
    arrivals |= {(2, rank): always for rank in (MATE, ACROSS, ACROSS_MATE)}
    arrivals |= {
        (0, SAME): has[0],
        (4, SAME): has[4],
        (0, MATE): has[0] & (core == 0),
        (4, MATE): has[4] & (core == 1),
        (0, ACROSS): has[0] & (y == 0),
        (4, ACROSS): has[4] & (y == 1),
        (0, ACROSS_MATE): has[0] & (y == 0),
        (4, ACROSS_MATE): has[4] & (y == 1),
    }

    def send(*key):
        way, plane, rank = key
        pl.when(plan[key])(lambda: halo_copy(way, slot_of[plane][rank]).start())

    def arrive(plane, rank):
        slot = slot_of[plane][rank]

        @pl.when(arrivals[plane, rank])
        def _():
            pltpu.make_async_remote_copy(
                src_ref=halo.at[slot],
                dst_ref=halo.at[slot],
                send_sem=halo_send.at[CORE, slot],
                recv_sem=halo_recv.at[slot],
                device_id={"chan": neighbours[CORE][0]},
                device_id_type=MESH,
            ).wait_recv()

    send(UP, 2, SAME)
    send(DOWN, 2, SAME)
    send(SIDE, 2, SAME)
    send(CORE, 2, SAME)

    for plane in (0, 1, 3, 4):

        @pl.when(jnp.logical_not(exists(plane)))
        def _():
            def clear(rank, _):
                halo[PLANE * plane + rank] = jnp.zeros((2, K1 * C, K2), jnp.bfloat16)
                return 0

            lax.fori_loop(0, PLANE, clear, 0)

    ownb[0] = jnp.broadcast_to(white_re.astype(jnp.float32)[:, None, :], (K1 * C, 8, K2))
    ownb[1] = jnp.broadcast_to(white_im.astype(jnp.float32)[:, None, :], (K1 * C, 8, K2))
    fetches[5].wait()

    def cross_terms(slots):
        total = jnp.zeros((64 * len(slots), LAGS), jnp.float32)
        for pair in range(K1 // 2):
            rows = slice(16 * pair, 16 * pair + 16)
            blocks = [
                (
                    halo[slot, 0, rows].astype(jnp.float32),
                    halo[slot, 1, rows].astype(jnp.float32),
                )
                for slot in slots
            ]
            for half in (0, 1):
                k1 = 2 * pair + half
                own_re, own_im = ownb[0, C * k1 : C * k1 + C], ownb[1, C * k1 : C * k1 + C]
                parts = []
                for block_re, block_im in blocks:
                    p_re = block_re[8 * half : 8 * half + 8][None]
                    p_im = block_im[8 * half : 8 * half + 8][None]
                    re = own_re * p_re + own_im * p_im
                    im = own_im * p_re - own_re * p_im
                    parts.append(
                        jnp.concatenate([re.reshape(64, K2), im.reshape(64, K2)], axis=1)
                    )
                cross = jnp.concatenate(parts, axis=0).astype(jnp.bfloat16)
                total += jnp.dot(cross, lag_ref[k1], preferred_element_type=jnp.float32)
        for index, slot in enumerate(slots):
            for c in range(C):
                value = total[64 * index + 8 * c : 64 * index + 8 * c + 8]
                acc[pl.ds(8 * (slot - r) + 7 - c, 8), c, :] = value

    def group_start(g):
        return group * g + 7 + (g >= wins // 2).astype(jnp.int32)

    def sums_copy(g):
        return pltpu.make_async_remote_copy(
            src_ref=sums_out.at[g],
            dst_ref=sums_in.at[w],
            send_sem=sums_send.at[g],
            recv_sem=sums_recv.at[w],
            device_id={"win": g},
            device_id_type=MESH,
        )

    def send_sums(first_group, count):
        def one(index, _):
            g = lax.rem(first_group + lax.rem(w + index, count), wins)

            @pl.when(g != w)
            def _():
                value = acc[pl.ds(group_start(g), group)]
                sums_out[g] = value.reshape(group * C, LAGS).astype(jnp.bfloat16)
                sums_copy(g).start()

            return 0

        lax.fori_loop(0, count, one, 0)

    far = [r + q + 12 * (r + q >= PLANE).astype(jnp.int32) for q in range(5)]
    units = [
        (own, own),
        (slot_of[2][MATE], slot_of[2][ACROSS]),
        (slot_of[2][ACROSS_MATE], slot_of[1][SAME]),
        (slot_of[3][SAME], slot_of[1][MATE]),
        (slot_of[3][MATE], slot_of[1][ACROSS]),
        (slot_of[3][ACROSS], slot_of[1][ACROSS_MATE]),
        (slot_of[3][ACROSS_MATE], far[0]),
        (far[1], far[2]),
        (far[3], far[4]),
    ]

    def before_1():
        arrive(2, ACROSS)
        send(UP, 2, ACROSS)
        send(DOWN, 2, ACROSS)
        send(CORE, 2, ACROSS)
        arrive(2, MATE)

    def before_2():
        arrive(1, SAME)
        send(UP, 1, SAME)
        send(CORE, 1, SAME)
        arrive(3, SAME)
        send(DOWN, 3, SAME)
        send(CORE, 3, SAME)
        arrive(2, ACROSS_MATE)

    def before_3():
        arrive(1, MATE)

    def before_4():
        arrive(1, ACROSS)
        send(UP, 1, ACROSS)
        send(CORE, 1, ACROSS)
        arrive(3, ACROSS)
        send(DOWN, 3, ACROSS)
        send(CORE, 3, ACROSS)
        arrive(3, MATE)

    def before_5():
        arrive(1, ACROSS_MATE)

    def before_6():
        arrive(0, SAME)
        send(CORE, 0, SAME)
        arrive(4, SAME)
        send(CORE, 4, SAME)
        arrive(3, ACROSS_MATE)
        arrive(0, MATE)
        arrive(0, ACROSS)

    def before_7():
        send(CORE, 0, ACROSS)
        arrive(4, ACROSS)
        send(CORE, 4, ACROSS)
        send_sums(2 - y, 5)
        arrive(4, MATE)
        arrive(0, ACROSS_MATE)
        arrive(4, ACROSS_MATE)

    events = {
        1: before_1,
        2: before_2,
        3: before_3,
        4: before_4,
        5: before_5,
        6: before_6,
        7: before_7,
    }

    def pick(u, values):
        chosen = values[0]
        for index in range(1, len(values)):
            chosen = jnp.where(u == index, values[index], chosen)
        return chosen

    def unit(u, _):
        for at, event in events.items():
            pl.when(u == at)(event)
        cross_terms([pick(u, [a for a, _ in units]), pick(u, [b for _, b in units])])
        return 0

    lax.fori_loop(0, len(units), unit, 0)
    send_sums(7 - y, 3)

    out_ref[...] = acc[pl.ds(group_start(w), group)]
    for (way, plane, rank), condition in plan.items():
        pl.when(condition)(halo_copy(way, slot_of[plane][rank]).wait_send)

    def gather(step, _):
        source = lax.rem(w + step, wins)
        pltpu.make_async_remote_copy(
            src_ref=sums_out.at[source],
            dst_ref=sums_in.at[source],
            send_sem=sums_send.at[source],
            recv_sem=sums_recv.at[source],
            device_id={"win": source},
            device_id_type=MESH,
        ).wait_recv()
        out_ref[...] += sums_in[source].astype(jnp.float32).reshape(group, C, LAGS)
        return 0

    lax.fori_loop(1, wins, gather, 0)

    def sent_sums(step, _):
        sums_copy(lax.rem(w + step, wins)).wait_send()
        return 0

    lax.fori_loop(1, wins, sent_sums, 0)


def solution(mesh):
    chans, wins = mesh.shape["chan"], mesh.shape["win"]
    group = BAND // wins

    def local(recordings, channel_live):
        constants = tables(wins * recordings.shape[0])
        operands = (channel_live, recordings, *constants)

        def body(*refs):
            kernel(chans, wins, *refs)

        copies = [pltpu.SMEM(channel_live.shape, channel_live.dtype)]
        copies += [pltpu.VMEM(array.shape, array.dtype) for array in operands[1:]]
        return pl.pallas_call(
            body,
            out_shape=jax.ShapeDtypeStruct((group, C, LAGS), jnp.float32),
            in_specs=[pl.BlockSpec(memory_space=pltpu.HBM)] * len(operands),
            out_specs=pl.BlockSpec(memory_space=pltpu.VMEM),
            scratch_shapes=[
                *copies,
                pltpu.VMEM((SLOTS, 2, K1 * C, K2), jnp.bfloat16),
                pltpu.VMEM((2, K1 * C, 8, K2), jnp.float32),
                pltpu.VMEM((BAND + 16, C, LAGS), jnp.float32),
                pltpu.VMEM((wins, group * C, LAGS), jnp.bfloat16),
                pltpu.VMEM((wins, group * C, LAGS), jnp.bfloat16),
                pltpu.SemaphoreType.DMA((len(operands),)),
                pltpu.SemaphoreType.DMA((4, SLOTS)),
                pltpu.SemaphoreType.DMA((SLOTS,)),
                pltpu.SemaphoreType.DMA((wins,)),
                pltpu.SemaphoreType.DMA((wins,)),
            ],
            compiler_params=pltpu.CompilerParams(
                collective_id=0, has_side_effects=True, vmem_limit_bytes=60 * 1024 * 1024
            ),
            name="correlate",
        )(*operands)

    return jax.shard_map(
        local,
        mesh=mesh,
        in_specs=(P("win", "chan", None), P("chan")),
        out_specs=P("win", "chan", None),
        check_vma=False,
    )
```

time: 40.8 us -> 27.2 us (0.67)
  the two profiles are of different devices: /device:TPU:32 before, /device:TPU:97 now
where the time goes in v2:
time: 27.2 us; the launch traced here: 26.8 us
  Pallas kernels  25.3 us (93%)
  local copies, waits for them, and re-layouts  1.47 us (5%)
    pallas_call x1, Pallas kernels, local(): pl.pallas_call(body, out_shape=jax.ShapeDtypeStruct((group, C, LAGS), jnp...  25.3 us
    unnamed x1, local copies, waits for them, and re-layouts  1.47 us

profile of v2, /device:TPU:97, one launch (start us, length us, event | category | flops | bytes accessed | tf_op | source)
XLA Modules:
  0.0 26.8 jit_solution(5000125740171146971)
XLA Ops:
  0.0 25.3 %correlate.1 = f32[16,8,128]{2,1,0:T(8,128)} custom-call(s32[8]{0:T(128)} %refs_0_.1, bf16[1,8,4096]{2,1,0:T(8,128)(2,1)} %refs_1_.1, bf16[256,128]{1,0:T(8,128)(2,1)} %constant.8.clone.refs_2_, f32[2,128,256]{2,1,0:T(8,128)} %constant.9.clone.refs_3_, bf16[2,512,128]{2,1,0:T(8,128)(2,1)} %constant.10.clone.refs_4_, bf16[16,256,128]{2,1,0:T(8,128)(2,1)} %constant.11.clone.refs_5_), custom_call_target="tpu_custom_call" | custom-call | tf_op jit(solution)/shard_map/correlate/pallas_call | solution.py:440
  25.3 1.5 %copy.8 = f32[16,8,128]{2,1,0:T(8,128)} copy(f32[16,8,128]{2,1,0:T(8,128)} %correlate.1) | data formatting | bytes 131072

commit v3 on v2

--- a/solution.py
+++ b/solution.py
@@ -1,3 +1,4 @@
+import functools
 import math
 
 import jax
@@ -21,9 +22,14 @@
 PLANE = 4
 PLANES = 5
 SLOTS = PLANE * PLANES
-UP, DOWN, SIDE, CORE = range(4)
 MESH = pl.DeviceIdType.MESH
-
+SAME, ACROSS = "same", "across"
+T1, A1, HERE = "t1", "a1", "here"
+ISSUE = [(T1, ACROSS), (T1, SAME), (A1, SAME), (HERE, ACROSS), (A1, ACROSS)]
+FAR = "far"
+NEAR = [(2, ACROSS), (1, SAME), (1, ACROSS), (3, SAME), (3, ACROSS)]
+NEAR_WAITS = [(1, SAME), (2, ACROSS), (1, ACROSS), (3, SAME), (3, ACROSS)]
+PLACES = [*NEAR, (0, SAME), (4, SAME), FAR]
 
 def bin_order():
     lane = np.arange(K2)
@@ -78,6 +84,8 @@
     sums_in,
     fetch_sem,
     halo_send,
+    mate_send,
+    relay_send,
     halo_recv,
     sums_send,
     sums_recv,
@@ -88,8 +96,7 @@
     planes = chans // PLANE
     z, r = j // PLANE, j % PLANE
     y, core = r // 2, r % 2
-    other = 1 - core
-    column, beside = 2 * y, 2 - 2 * y
+    beside = 2 - 2 * y
     own = 2 * PLANE + r
 
     fetches = [
@@ -105,18 +112,22 @@
             )
         )
     ]
-    for fetch in fetches:
-        fetch.start()
 
     def exists(plane):
         there = z + plane - 2
         return (there >= 0) & (there < planes)
 
-    neighbours = {
-        UP: (j + PLANE, -PLANE),
-        DOWN: (j - PLANE, PLANE),
-        SIDE: (j + 2 - 4 * y, 0),
-        CORE: (j + 1 - 2 * core, 0),
+    side, mate = j + 2 - 4 * y, j + 1 - 2 * core
+    towards = 2 * y - 1
+    always = j >= 0
+    has = [exists(plane) for plane in range(PLANES)]
+    has_t1, has_a1 = (has[1] & (y == 0)) | (has[3] & (y == 1)), (has[3] & (y == 0)) | (has[1] & (y == 1))
+    targets = {
+        (T1, SAME): (-towards, j, has_a1),
+        (A1, SAME): (towards, j, has_t1),
+        (HERE, ACROSS): (0, side, always),
+        (T1, ACROSS): (towards, side, has_t1),
+        (A1, ACROSS): (-towards, side, has_a1),
     }
 
     barrier = pltpu.get_barrier_semaphore()
@@ -124,10 +135,13 @@
     def greet(there):
         pl.semaphore_signal(barrier, inc=1, device_id=there, device_id_type=MESH)
 
-    pl.when(exists(3))(lambda: greet({"chan": j + PLANE}))
-    pl.when(exists(1))(lambda: greet({"chan": j - PLANE}))
-    greet({"chan": neighbours[SIDE][0]})
-    greet({"chan": neighbours[CORE][0]})
+    greeted = 1 + (wins - 1)
+    greet({"chan": mate})
+    for up, there, present in targets.values():
+        pl.when(present)(lambda: greet({"chan": there + PLANE * up}))
+        greeted += present.astype(jnp.int32)
+    for fetch in fetches:
+        fetch.start()
     for d in range(1, wins):
         greet({"win": lax.rem(w + d, wins)})
 
@@ -163,82 +177,68 @@
     halo[own, 0] = white_re
     halo[own, 1] = white_im
 
-    beyond = exists(1).astype(jnp.int32) + exists(3).astype(jnp.int32)
-    pl.semaphore_wait(barrier, beyond + 2 + (wins - 1))
-
-    def halo_copy(way, slot):
-        there, shift = neighbours[way]
+    pl.semaphore_wait(barrier, greeted)
+
+    far_plane = 2 + 2 * towards
+    slot_of = {
+        place: PLANE * place[0] + (r if place[1] == SAME else beside + core) for place in PLACES[:-1]
+    }
+    slot_of[FAR] = PLANE * far_plane + beside + core
+    to_mate = mate - j
+    arrives = {place: has[place[0]] for place in PLACES[:-1]}
+    arrives[FAR] = (has[0] & (y == 0)) | (has[4] & (y == 1))
+    passed_on, from_mate = dict(arrives), dict(arrives)
+    passed_on[0, SAME] = has[0] & (core == 1)
+    from_mate[0, SAME] = has[0] & (core == 0)
+    passed_on[4, SAME] = has[4] & (core == 0)
+    from_mate[4, SAME] = has[4] & (core == 1)
+    pair_of = {place: slot_of[place] + to_mate for place in PLACES}
+    pair_of[0, SAME] = slot_of[0, SAME] + jnp.where(core == 0, to_mate, 0)
+    pair_of[4, SAME] = slot_of[4, SAME] + jnp.where(core == 1, to_mate, 0)
+
+    def out_copy(place):
+        up, there, _ = targets[place]
+        return pltpu.make_async_remote_copy(
+            src_ref=halo.at[own],
+            dst_ref=halo.at[own - PLANE * up],
+            send_sem=halo_send.at[ISSUE.index(place)],
+            recv_sem=halo_recv.at[own - PLANE * up],
+            device_id={"chan": there + PLANE * up},
+            device_id_type=MESH,
+        )
+
+    inside = has[1] & has[3]
+    relays = {
+        (1, SAME): (1, inside),
+        (3, SAME): (-1, inside),
+        (1, ACROSS): (1, inside & (y == 0)),
+        (3, ACROSS): (-1, inside & (y == 1)),
+    }
+
+    def relay_copy(place):
+        up, slot = relays[place][0], slot_of[place]
         return pltpu.make_async_remote_copy(
             src_ref=halo.at[slot],
-            dst_ref=halo.at[slot + shift],
-            send_sem=halo_send.at[way, slot],
-            recv_sem=halo_recv.at[slot + shift],
-            device_id={"chan": there},
+            dst_ref=halo.at[slot - PLANE * up],
+            send_sem=relay_send.at[PLACES.index(place)],
+            recv_sem=halo_recv.at[slot - PLANE * up],
+            device_id={"chan": j + PLANE * up},
             device_id_type=MESH,
         )
 
-    always = j >= 0
-    has = [exists(plane) for plane in range(PLANES)]
-    inside = has[1] & has[3]
-    same, across = column + core, beside + core
-    slot_of = [[PLANE * plane + rank for rank in (same, column + other, across, beside + other)] for plane in range(PLANES)]
-    SAME, MATE, ACROSS, ACROSS_MATE = range(4)
-    plan = {
-        (UP, 2, SAME): has[3],
-        (DOWN, 2, SAME): has[1],
-        (SIDE, 2, SAME): always,
-        (CORE, 2, SAME): always,
-        (UP, 2, ACROSS): has[3],
-        (DOWN, 2, ACROSS): has[1],
-        (CORE, 2, ACROSS): always,
-        (UP, 1, SAME): inside,
-        (CORE, 1, SAME): has[1],
-        (DOWN, 3, SAME): inside,
-        (CORE, 3, SAME): has[3],
-        (UP, 1, ACROSS): inside & (y == 0),
-        (CORE, 1, ACROSS): has[1],
-        (DOWN, 3, ACROSS): inside & (y == 1),
-        (CORE, 3, ACROSS): has[3],
-        (CORE, 0, SAME): has[0] & (core == 1),
-        (CORE, 4, SAME): has[4] & (core == 0),
-        (CORE, 0, ACROSS): has[0] & (y == 0),
-        (CORE, 4, ACROSS): has[4] & (y == 1),
-    }
-    arrivals = {(plane, rank): has[plane] for plane in (1, 3) for rank in range(4)}
-    arrivals |= {(2, rank): always for rank in (MATE, ACROSS, ACROSS_MATE)}
-    arrivals |= {
-        (0, SAME): has[0],
-        (4, SAME): has[4],
-        (0, MATE): has[0] & (core == 0),
-        (4, MATE): has[4] & (core == 1),
-        (0, ACROSS): has[0] & (y == 0),
-        (4, ACROSS): has[4] & (y == 1),
-        (0, ACROSS_MATE): has[0] & (y == 0),
-        (4, ACROSS_MATE): has[4] & (y == 1),
-    }
-
-    def send(*key):
-        way, plane, rank = key
-        pl.when(plan[key])(lambda: halo_copy(way, slot_of[plane][rank]).start())
-
-    def arrive(plane, rank):
-        slot = slot_of[plane][rank]
-
-        @pl.when(arrivals[plane, rank])
-        def _():
-            pltpu.make_async_remote_copy(
-                src_ref=halo.at[slot],
-                dst_ref=halo.at[slot],
-                send_sem=halo_send.at[CORE, slot],
-                recv_sem=halo_recv.at[slot],
-                device_id={"chan": neighbours[CORE][0]},
-                device_id_type=MESH,
-            ).wait_recv()
-
-    send(UP, 2, SAME)
-    send(DOWN, 2, SAME)
-    send(SIDE, 2, SAME)
-    send(CORE, 2, SAME)
+    def mate_copy(slot):
+        return pltpu.make_async_remote_copy(
+            src_ref=halo.at[slot],
+            dst_ref=halo.at[slot],
+            send_sem=mate_send.at[slot],
+            recv_sem=halo_recv.at[slot],
+            device_id={"chan": mate},
+            device_id_type=MESH,
+        )
+
+    for place in ISSUE:
+        pl.when(targets[place][2])(lambda: out_copy(place).start())
+    mate_copy(own).start()
 
     for plane in (0, 1, 3, 4):
 
@@ -299,7 +299,7 @@
 
     def send_sums(first_group, count):
         def one(index, _):
-            g = lax.rem(first_group + lax.rem(w + index, count), wins)
+            g = first_group + lax.rem(w + index, count)
 
             @pl.when(g != w)
             def _():
@@ -311,77 +311,56 @@
 
         lax.fori_loop(0, count, one, 0)
 
-    far = [r + q + 12 * (r + q >= PLANE).astype(jnp.int32) for q in range(5)]
-    units = [
-        (own, own),
-        (slot_of[2][MATE], slot_of[2][ACROSS]),
-        (slot_of[2][ACROSS_MATE], slot_of[1][SAME]),
-        (slot_of[3][SAME], slot_of[1][MATE]),
-        (slot_of[3][MATE], slot_of[1][ACROSS]),
-        (slot_of[3][ACROSS], slot_of[1][ACROSS_MATE]),
-        (slot_of[3][ACROSS_MATE], far[0]),
-        (far[1], far[2]),
-        (far[3], far[4]),
-    ]
-
-    def before_1():
-        arrive(2, ACROSS)
-        send(UP, 2, ACROSS)
-        send(DOWN, 2, ACROSS)
-        send(CORE, 2, ACROSS)
-        arrive(2, MATE)
-
-    def before_2():
-        arrive(1, SAME)
-        send(UP, 1, SAME)
-        send(CORE, 1, SAME)
-        arrive(3, SAME)
-        send(DOWN, 3, SAME)
-        send(CORE, 3, SAME)
-        arrive(2, ACROSS_MATE)
-
-    def before_3():
-        arrive(1, MATE)
-
-    def before_4():
-        arrive(1, ACROSS)
-        send(UP, 1, ACROSS)
-        send(CORE, 1, ACROSS)
-        arrive(3, ACROSS)
-        send(DOWN, 3, ACROSS)
-        send(CORE, 3, ACROSS)
-        arrive(3, MATE)
-
-    def before_5():
-        arrive(1, ACROSS_MATE)
-
-    def before_6():
-        arrive(0, SAME)
-        send(CORE, 0, SAME)
-        arrive(4, SAME)
-        send(CORE, 4, SAME)
-        arrive(3, ACROSS_MATE)
-        arrive(0, MATE)
-        arrive(0, ACROSS)
-
-    def before_7():
-        send(CORE, 0, ACROSS)
-        arrive(4, ACROSS)
-        send(CORE, 4, ACROSS)
-        send_sums(2 - y, 5)
-        arrive(4, MATE)
-        arrive(0, ACROSS_MATE)
-        arrive(4, ACROSS_MATE)
-
-    events = {
-        1: before_1,
-        2: before_2,
-        3: before_3,
-        4: before_4,
-        5: before_5,
-        6: before_6,
-        7: before_7,
-    }
+    def by_column(first, second):
+        return jnp.where(y == 0, first, second)
+
+    def either(conditions, first, second):
+        return (conditions[first] & (y == 0)) | (conditions[second] & (y == 1))
+
+    last = [(FAR, (4, SAME)), ((4, SAME), FAR)]
+    units = [(own, own + to_mate)] + [(slot_of[place], pair_of[place]) for place in [*NEAR, (0, SAME)]]
+    units += [(by_column(slot_of[a], slot_of[b]), by_column(pair_of[a], pair_of[b])) for a, b in last]
+
+    def from_chip(place):
+        pl.when(arrives[place])(lambda: mate_copy(slot_of[place]).wait_recv())
+        if place in relays:
+            pl.when(relays[place][1])(lambda: relay_copy(place).start())
+        pl.when(passed_on[place])(lambda: mate_copy(slot_of[place]).start())
+
+    def last_from_chip(index):
+        slot = by_column(*(slot_of[place] for place in last[index]))
+        pl.when(either(arrives, *last[index]))(lambda: mate_copy(slot).wait_recv())
+        pl.when(either(passed_on, *last[index]))(lambda: mate_copy(slot).start())
+
+    def from_core(place):
+        pl.when(from_mate[place])(lambda: mate_copy(slot_of[place] + to_mate).wait_recv())
+
+    def last_from_core(index):
+        slot = by_column(*(slot_of[place] for place in last[index])) + to_mate
+        pl.when(either(from_mate, *last[index]))(lambda: mate_copy(slot).wait_recv())
+
+    def before(u):
+        if u == 0:
+            mate_copy(own + to_mate).wait_recv()
+        elif u <= len(NEAR):
+            if u == 1:
+                for place in NEAR_WAITS:
+                    from_chip(place)
+            from_core(NEAR[u - 1])
+        elif u == 6:
+            from_chip((0, SAME))
+            send_sums(2 - y, 5)
+            last_from_chip(0)
+            from_core((0, SAME))
+        elif u == 7:
+            send_sums(0, y)
+            last_from_chip(1)
+            last_from_core(0)
+        else:
+            send_sums(0, 2 - 2 * y)
+            last_from_core(1)
+
+    events = {u: functools.partial(before, u) for u in range(len(units))}
 
     def pick(u, values):
         chosen = values[0]
@@ -396,11 +375,17 @@
         return 0
 
     lax.fori_loop(0, len(units), unit, 0)
-    send_sums(7 - y, 3)
+
+    send_sums(7 - y, 1 + y)
 
     out_ref[...] = acc[pl.ds(group_start(w), group)]
-    for (way, plane, rank), condition in plan.items():
-        pl.when(condition)(halo_copy(way, slot_of[plane][rank]).wait_send)
+    for place in relays:
+        pl.when(relays[place][1])(lambda: relay_copy(place).wait_send())
+    for place in targets:
+        pl.when(targets[place][2])(lambda: out_copy(place).wait_send())
+    for place in PLACES:
+        pl.when(passed_on[place])(lambda: mate_copy(slot_of[place]).wait_send())
+    mate_copy(own).wait_send()
 
     def gather(step, _):
         source = lax.rem(w + step, wins)
@@ -431,6 +416,7 @@
     def local(recordings, channel_live):
         constants = tables(wins * recordings.shape[0])
         operands = (channel_live, recordings, *constants)
+        operands = [pltpu.with_memory_space_constraint(array, pltpu.HBM) for array in operands]
 
         def body(*refs):
             kernel(chans, wins, *refs)
@@ -439,7 +425,7 @@
         copies += [pltpu.VMEM(array.shape, array.dtype) for array in operands[1:]]
         return pl.pallas_call(
             body,
-            out_shape=jax.ShapeDtypeStruct((group, C, LAGS), jnp.float32),
+            out_shape=pltpu.VMEM((group, C, LAGS), jnp.float32),
             in_specs=[pl.BlockSpec(memory_space=pltpu.HBM)] * len(operands),
             out_specs=pl.BlockSpec(memory_space=pltpu.VMEM),
             scratch_shapes=[
@@ -450,13 +436,15 @@
                 pltpu.VMEM((wins, group * C, LAGS), jnp.bfloat16),
                 pltpu.VMEM((wins, group * C, LAGS), jnp.bfloat16),
                 pltpu.SemaphoreType.DMA((len(operands),)),
-                pltpu.SemaphoreType.DMA((4, SLOTS)),
+                pltpu.SemaphoreType.DMA((8,)),
+                pltpu.SemaphoreType.DMA((SLOTS,)),
+                pltpu.SemaphoreType.DMA((8,)),
                 pltpu.SemaphoreType.DMA((SLOTS,)),
                 pltpu.SemaphoreType.DMA((wins,)),
                 pltpu.SemaphoreType.DMA((wins,)),
             ],
             compiler_params=pltpu.CompilerParams(
-                collective_id=0, has_side_effects=True, vmem_limit_bytes=60 * 1024 * 1024
+                collective_id=0, has_side_effects=True, vmem_limit_bytes=24 * 1024 * 1024
             ),
             name="correlate",
         )(*operands)

time: 27.2 us -> 24.3 us (0.89)
  the two profiles are of different devices: /device:TPU:97 before, /device:TPU:127 now
where the time goes in v3:
time: 24.3 us; the launch traced here: 24.2 us
  Pallas kernels  23.6 us (97%)
  local copies, waits for them, and re-layouts  0.63 us (3%)
    pallas_call x1, Pallas kernels, local(): pl.pallas_call(body, out_shape=pltpu.VMEM((group, C, LAGS), jnp.float32),...  23.6 us
    unnamed x1, local copies, waits for them, and re-layouts  0.63 us

profile of v3, /device:TPU:127, one launch (start us, length us, event | category | flops | bytes accessed | tf_op | source)
XLA Modules:
  0.0 24.2 jit_solution(17705263255710245046)
XLA Ops:
  0.0 23.6 %correlate.1 = f32[16,8,128]{2,1,0:T(8,128)S(1)} custom-call(s32[8]{0:T(128)} %refs_0_.1, bf16[1,8,4096]{2,1,0:T(8,128)(2,1)} %refs_1_.1, bf16[256,128]{1,0:T(8,128)(2,1)} %constant.8.clone.refs_2_, f32[2,128,256]{2,1,0:T(8,128)} %constant.9.clone.refs_3_, bf16[2,512,128]{2,1,0:T(8,128)(2,1)} %constant.10.clone.refs_4_, ...), custom_call_target="tpu_custom_call" | custom-call | tf_op jit(solution)/shard_map/correlate/pallas_call | solution.py:426
  23.6 0.6 %copy.8 = f32[16,8,128]{2,1,0:T(8,128)} copy(f32[16,8,128]{2,1,0:T(8,128)S(1)} %correlate.1) | data formatting | bytes 131072

commit v4 on v3

--- a/solution.py
+++ b/solution.py
@@ -20,6 +20,7 @@
 K1 = 16
 K2 = 128
 PLANE = 4
+WIN_X = 4
 PLANES = 5
 SLOTS = PLANE * PLANES
 MESH = pl.DeviceIdType.MESH
@@ -89,6 +90,8 @@
     halo_recv,
     sums_send,
     sums_recv,
+    row_in,
+    rest_in,
 ):
     j = lax.axis_index("chan")
     w = lax.axis_index("win")
@@ -130,20 +133,25 @@
         (A1, ACROSS): (-towards, side, has_a1),
     }
 
+    fetches[0].start()
+    fetches[1].start()
     barrier = pltpu.get_barrier_semaphore()
 
     def greet(there):
         pl.semaphore_signal(barrier, inc=1, device_id=there, device_id_type=MESH)
 
-    greeted = 1 + (wins - 1)
+    row, row_width = w // WIN_X * WIN_X, WIN_X
+    beside_x = [row + lax.rem(w + step, row_width) for step in (1, row_width - 1)]
+    beyond_y = lax.rem(w + WIN_X, wins)
+    greeted = 1 + 3
     greet({"chan": mate})
     for up, there, present in targets.values():
         pl.when(present)(lambda: greet({"chan": there + PLANE * up}))
         greeted += present.astype(jnp.int32)
-    for fetch in fetches:
+    for there in (*beside_x, beyond_y):
+        greet({"win": there})
+    for fetch in fetches[2:]:
         fetch.start()
-    for d in range(1, wins):
-        greet({"win": lax.rem(w + d, wins)})
 
     fetches[0].wait()
     fetches[1].wait()
@@ -240,6 +248,12 @@
         pl.when(targets[place][2])(lambda: out_copy(place).start())
     mate_copy(own).start()
 
+    def tell(semaphore, there):
+        pl.semaphore_signal(semaphore, inc=1, device_id={"win": there}, device_id_type=MESH)
+
+    for there in beside_x:
+        tell(row_in, there)
+
     for plane in (0, 1, 3, 4):
 
         @pl.when(jnp.logical_not(exists(plane)))
@@ -346,9 +360,12 @@
             if u == 1:
                 for place in NEAR_WAITS:
                     from_chip(place)
+                pl.semaphore_wait(row_in, 2)
+                tell(rest_in, beyond_y)
             from_core(NEAR[u - 1])
         elif u == 6:
             from_chip((0, SAME))
+            pl.semaphore_wait(rest_in, 1)
             send_sums(2 - y, 5)
             last_from_chip(0)
             from_core((0, SAME))
@@ -442,6 +459,8 @@
                 pltpu.SemaphoreType.DMA((SLOTS,)),
                 pltpu.SemaphoreType.DMA((wins,)),
                 pltpu.SemaphoreType.DMA((wins,)),
+                pltpu.SemaphoreType.REGULAR,
+                pltpu.SemaphoreType.REGULAR,
             ],
             compiler_params=pltpu.CompilerParams(
                 collective_id=0, has_side_effects=True, vmem_limit_bytes=24 * 1024 * 1024

time: 24.3 us -> 23 us (0.947)
  the two profiles are of different devices: /device:TPU:127 before, /device:TPU:65 now
where the time goes in v4:
time: 23 us; the launch traced here: 22.9 us
  Pallas kernels  22.3 us (97%)
  local copies, waits for them, and re-layouts  0.63 us (3%)
    pallas_call x1, Pallas kernels, local(): pl.pallas_call(body, out_shape=pltpu.VMEM((group, C, LAGS), jnp.float32),...  22.3 us
    unnamed x1, local copies, waits for them, and re-layouts  0.63 us

profile of v4, /device:TPU:65, one launch (start us, length us, event | category | flops | bytes accessed | tf_op | source)
XLA Modules:
  0.0 22.9 jit_solution(14343668807787352429)
XLA Ops:
  0.0 22.3 %correlate.1 = f32[16,8,128]{2,1,0:T(8,128)S(1)} custom-call(s32[8]{0:T(128)} %refs_0_.1, bf16[1,8,4096]{2,1,0:T(8,128)(2,1)} %refs_1_.1, bf16[256,128]{1,0:T(8,128)(2,1)} %constant.8.clone.refs_2_, f32[2,128,256]{2,1,0:T(8,128)} %constant.9.clone.refs_3_, bf16[2,512,128]{2,1,0:T(8,128)(2,1)} %constant.10.clone.refs_4_, ...), custom_call_target="tpu_custom_call" | custom-call | tf_op jit(solution)/shard_map/correlate/pallas_call | solution.py:443
  22.3 0.6 %copy.8 = f32[16,8,128]{2,1,0:T(8,128)} copy(f32[16,8,128]{2,1,0:T(8,128)S(1)} %correlate.1) | data formatting | bytes 131072

commit v5 on v4

--- a/solution.py
+++ b/solution.py
@@ -26,11 +26,9 @@
 MESH = pl.DeviceIdType.MESH
 SAME, ACROSS = "same", "across"
 T1, A1, HERE = "t1", "a1", "here"
-ISSUE = [(T1, ACROSS), (T1, SAME), (A1, SAME), (HERE, ACROSS), (A1, ACROSS)]
+ISSUE = [(T1, SAME), (A1, SAME), (T1, ACROSS), (HERE, ACROSS)]
 FAR = "far"
-NEAR = [(2, ACROSS), (1, SAME), (1, ACROSS), (3, SAME), (3, ACROSS)]
-NEAR_WAITS = [(1, SAME), (2, ACROSS), (1, ACROSS), (3, SAME), (3, ACROSS)]
-PLACES = [*NEAR, (0, SAME), (4, SAME), FAR]
+PLACES = [(2, ACROSS), (1, SAME), (1, ACROSS), (3, SAME), (3, ACROSS), (0, SAME), (4, SAME), FAR]
 
 def bin_order():
     lane = np.arange(K2)
@@ -130,7 +128,6 @@
         (A1, SAME): (towards, j, has_t1),
         (HERE, ACROSS): (0, side, always),
         (T1, ACROSS): (towards, side, has_t1),
-        (A1, ACROSS): (-towards, side, has_a1),
     }
 
     fetches[0].start()
@@ -144,12 +141,12 @@
     beside_x = [row + lax.rem(w + step, row_width) for step in (1, row_width - 1)]
     beyond_y = lax.rem(w + WIN_X, wins)
     greeted = 1 + 3
-    greet({"chan": mate})
+    for there in (beyond_y, *beside_x):
+        greet({"win": there})
     for up, there, present in targets.values():
         pl.when(present)(lambda: greet({"chan": there + PLANE * up}))
         greeted += present.astype(jnp.int32)
-    for there in (*beside_x, beyond_y):
-        greet({"win": there})
+    greet({"chan": mate})
     for fetch in fetches[2:]:
         fetch.start()
 
@@ -221,14 +218,14 @@
         (3, SAME): (-1, inside),
         (1, ACROSS): (1, inside & (y == 0)),
         (3, ACROSS): (-1, inside & (y == 1)),
+        (2, ACROSS): (towards, has_t1),
     }
 
-    def relay_copy(place):
-        up, slot = relays[place][0], slot_of[place]
+    def relay_copy(slot, up):
         return pltpu.make_async_remote_copy(
             src_ref=halo.at[slot],
             dst_ref=halo.at[slot - PLANE * up],
-            send_sem=relay_send.at[PLACES.index(place)],
+            send_sem=relay_send.at[slot],
             recv_sem=halo_recv.at[slot - PLANE * up],
             device_id={"chan": j + PLANE * up},
             device_id_type=MESH,
@@ -325,59 +322,65 @@
 
         lax.fori_loop(0, count, one, 0)
 
-    def by_column(first, second):
-        return jnp.where(y == 0, first, second)
-
-    def either(conditions, first, second):
-        return (conditions[first] & (y == 0)) | (conditions[second] & (y == 1))
-
-    last = [(FAR, (4, SAME)), ((4, SAME), FAR)]
-    units = [(own, own + to_mate)] + [(slot_of[place], pair_of[place]) for place in [*NEAR, (0, SAME)]]
-    units += [(by_column(slot_of[a], slot_of[b]), by_column(pair_of[a], pair_of[b])) for a, b in last]
-
     def from_chip(place):
         pl.when(arrives[place])(lambda: mate_copy(slot_of[place]).wait_recv())
         if place in relays:
-            pl.when(relays[place][1])(lambda: relay_copy(place).start())
+            pl.when(relays[place][1])(lambda: relay_copy(slot_of[place], relays[place][0]).start())
         pl.when(passed_on[place])(lambda: mate_copy(slot_of[place]).start())
-
-    def last_from_chip(index):
-        slot = by_column(*(slot_of[place] for place in last[index]))
-        pl.when(either(arrives, *last[index]))(lambda: mate_copy(slot).wait_recv())
-        pl.when(either(passed_on, *last[index]))(lambda: mate_copy(slot).start())
 
     def from_core(place):
         pl.when(from_mate[place])(lambda: mate_copy(slot_of[place] + to_mate).wait_recv())
 
-    def last_from_core(index):
-        slot = by_column(*(slot_of[place] for place in last[index])) + to_mate
-        pl.when(either(from_mate, *last[index]))(lambda: mate_copy(slot).wait_recv())
-
-    def before(u):
+    def rest_is_in():
+        pl.semaphore_wait(rest_in, 1)
+
+    def row_is_in():
+        pl.semaphore_wait(row_in, 2)
+        tell(rest_in, beyond_y)
+
+    chip, core_of, sums = (
+        lambda *places: [functools.partial(from_chip, place) for place in places],
+        lambda place: [functools.partial(from_core, place)],
+        lambda first, count: [functools.partial(send_sums, first, count)],
+    )
+    steps = (
+        [(2, ACROSS), (1, SAME), (1, ACROSS), (3, SAME), (0, SAME), FAR, (3, ACROSS), (4, SAME)],
+        [(2, ACROSS), (3, SAME), (3, ACROSS), (1, SAME), (1, ACROSS), (0, SAME), (4, SAME), FAR],
+    )
+    before = (
+        {
+            1: [row_is_in, *chip((1, SAME), (2, ACROSS), (1, ACROSS), (3, SAME))],
+            4: [rest_is_in, *sums(2, 3)],
+            5: [*chip((0, SAME)), *sums(5, 1)],
+            6: chip(FAR, (3, ACROSS)),
+            7: [*sums(0, 2), *chip((4, SAME))],
+            8: sums(6, 1),
+        },
+        {
+            1: [row_is_in, *chip((3, SAME), (2, ACROSS), (3, ACROSS), (1, SAME))],
+            4: [*chip((1, ACROSS)), rest_is_in, *sums(3, 3)],
+            6: [*chip((0, SAME)), *sums(1, 2), *chip((4, SAME))],
+            7: [*sums(0, 1), *chip(FAR)],
+        },
+    )
+
+    def event(u, column):
         if u == 0:
             mate_copy(own + to_mate).wait_recv()
-        elif u <= len(NEAR):
-            if u == 1:
-                for place in NEAR_WAITS:
-                    from_chip(place)
-                pl.semaphore_wait(row_in, 2)
-                tell(rest_in, beyond_y)
-            from_core(NEAR[u - 1])
-        elif u == 6:
-            from_chip((0, SAME))
-            pl.semaphore_wait(rest_in, 1)
-            send_sums(2 - y, 5)
-            last_from_chip(0)
-            from_core((0, SAME))
-        elif u == 7:
-            send_sums(0, y)
-            last_from_chip(1)
-            last_from_core(0)
         else:
-            send_sums(0, 2 - 2 * y)
-            last_from_core(1)
-
-    events = {u: functools.partial(before, u) for u in range(len(units))}
+            for act in [*before[column].get(u, []), *core_of(steps[column][u - 1])]:
+                act()
+
+    def before_step(u):
+        for column in (0, 1):
+            pl.when(y == column)(functools.partial(event, u, column))
+
+    units = [(own, own + to_mate)]
+    units += [
+        tuple(jnp.where(y == 0, table[a], table[b]) for table in (slot_of, pair_of))
+        for a, b in zip(*steps, strict=True)
+    ]
+    events = {u: functools.partial(before_step, u) for u in range(len(units))}
 
     def pick(u, values):
         chosen = values[0]
@@ -397,7 +400,7 @@
 
     out_ref[...] = acc[pl.ds(group_start(w), group)]
     for place in relays:
-        pl.when(relays[place][1])(lambda: relay_copy(place).wait_send())
+        pl.when(relays[place][1])(lambda: relay_copy(slot_of[place], relays[place][0]).wait_send())
     for place in targets:
         pl.when(targets[place][2])(lambda: out_copy(place).wait_send())
     for place in PLACES:
@@ -455,7 +458,7 @@
                 pltpu.SemaphoreType.DMA((len(operands),)),
                 pltpu.SemaphoreType.DMA((8,)),
                 pltpu.SemaphoreType.DMA((SLOTS,)),
-                pltpu.SemaphoreType.DMA((8,)),
+                pltpu.SemaphoreType.DMA((SLOTS,)),
                 pltpu.SemaphoreType.DMA((SLOTS,)),
                 pltpu.SemaphoreType.DMA((wins,)),
                 pltpu.SemaphoreType.DMA((wins,)),

time: 23 us -> 22.6 us (0.983)
  the two profiles are of different devices: /device:TPU:65 before, /device:TPU:97 now
where the time goes in v5:
time: 22.6 us; the launch traced here: 22.3 us
  Pallas kernels  21.7 us (96%)
  local copies, waits for them, and re-layouts  0.63 us (3%)
    pallas_call x1, Pallas kernels, local(): pl.pallas_call(body, out_shape=pltpu.VMEM((group, C, LAGS), jnp.float32),...  21.7 us
    unnamed x1, local copies, waits for them, and re-layouts  0.63 us

profile of v5, /device:TPU:97, one launch (start us, length us, event | category | flops | bytes accessed | tf_op | source)
XLA Modules:
  0.0 22.3 jit_solution(7983210359463101976)
XLA Ops:
  0.0 21.7 %correlate.1 = f32[16,8,128]{2,1,0:T(8,128)S(1)} custom-call(s32[8]{0:T(128)} %refs_0_.1, bf16[1,8,4096]{2,1,0:T(8,128)(2,1)} %refs_1_.1, bf16[256,128]{1,0:T(8,128)(2,1)} %constant.8.clone.refs_2_, f32[2,128,256]{2,1,0:T(8,128)} %constant.9.clone.refs_3_, bf16[2,512,128]{2,1,0:T(8,128)(2,1)} %constant.10.clone.refs_4_, ...), custom_call_target="tpu_custom_call" | custom-call | tf_op jit(solution)/shard_map/correlate/pallas_call | solution.py:446
  21.7 0.6 %copy.8 = f32[16,8,128]{2,1,0:T(8,128)} copy(f32[16,8,128]{2,1,0:T(8,128)S(1)} %correlate.1) | data formatting | bytes 131072

commit v6 on v5

--- a/solution.py
+++ b/solution.py
@@ -26,7 +26,7 @@
 MESH = pl.DeviceIdType.MESH
 SAME, ACROSS = "same", "across"
 T1, A1, HERE = "t1", "a1", "here"
-ISSUE = [(T1, SAME), (A1, SAME), (T1, ACROSS), (HERE, ACROSS)]
+ISSUE = [(T1, ACROSS), (T1, SAME), (A1, SAME), (HERE, ACROSS)]
 FAR = "far"
 PLACES = [(2, ACROSS), (1, SAME), (1, ACROSS), (3, SAME), (3, ACROSS), (0, SAME), (4, SAME), FAR]
 
@@ -124,10 +124,10 @@
     has = [exists(plane) for plane in range(PLANES)]
     has_t1, has_a1 = (has[1] & (y == 0)) | (has[3] & (y == 1)), (has[3] & (y == 0)) | (has[1] & (y == 1))
     targets = {
+        (T1, ACROSS): (towards, side, has_t1),
         (T1, SAME): (-towards, j, has_a1),
         (A1, SAME): (towards, j, has_t1),
         (HERE, ACROSS): (0, side, always),
-        (T1, ACROSS): (towards, side, has_t1),
     }
 
     fetches[0].start()
@@ -141,11 +141,11 @@
     beside_x = [row + lax.rem(w + step, row_width) for step in (1, row_width - 1)]
     beyond_y = lax.rem(w + WIN_X, wins)
     greeted = 1 + 3
-    for there in (beyond_y, *beside_x):
-        greet({"win": there})
     for up, there, present in targets.values():
         pl.when(present)(lambda: greet({"chan": there + PLANE * up}))
         greeted += present.astype(jnp.int32)
+    for there in (beyond_y, *beside_x):
+        greet({"win": there})
     greet({"chan": mate})
     for fetch in fetches[2:]:
         fetch.start()
@@ -308,9 +308,9 @@
             device_id_type=MESH,
         )
 
-    def send_sums(first_group, count):
+    def send_sums(first_group, count, turned=True):
         def one(index, _):
-            g = first_group + lax.rem(w + index, count)
+            g = first_group + (lax.rem(w + index, count) if turned else index)
 
             @pl.when(g != w)
             def _():
@@ -353,7 +353,7 @@
             4: [rest_is_in, *sums(2, 3)],
             5: [*chip((0, SAME)), *sums(5, 1)],
             6: chip(FAR, (3, ACROSS)),
-            7: [*sums(0, 2), *chip((4, SAME))],
+            7: [functools.partial(send_sums, 0, 2, turned=False), *chip((4, SAME))],
             8: sums(6, 1),
         },
         {
@@ -396,7 +396,8 @@
 
     lax.fori_loop(0, len(units), unit, 0)
 
-    send_sums(7 - y, 1 + y)
+    send_sums(7, 1)
+    send_sums(6, y)
 
     out_ref[...] = acc[pl.ds(group_start(w), group)]
     for place in relays:
@@ -406,6 +407,12 @@
     for place in PLACES:
         pl.when(passed_on[place])(lambda: mate_copy(slot_of[place]).wait_send())
     mate_copy(own).wait_send()
+
+    def sent_sums(step, _):
+        sums_copy(lax.rem(w + step, wins)).wait_send()
+        return 0
+
+    lax.fori_loop(1, wins, sent_sums, 0)
 
     def gather(step, _):
         source = lax.rem(w + step, wins)
@@ -421,12 +428,6 @@
         return 0
 
     lax.fori_loop(1, wins, gather, 0)
-
-    def sent_sums(step, _):
-        sums_copy(lax.rem(w + step, wins)).wait_send()
-        return 0
-
-    lax.fori_loop(1, wins, sent_sums, 0)
 
 
 def solution(mesh):

time: 22.6 us -> 22.4 us (level)
  no operation moved by 1% of the time
where the time goes in v6:
time: 22.4 us; the launch traced here: 22.3 us
  Pallas kernels  21.7 us (97%)
  local copies, waits for them, and re-layouts  0.63 us (3%)
    pallas_call x1, Pallas kernels, local(): pl.pallas_call(body, out_shape=pltpu.VMEM((group, C, LAGS), jnp.float32),...  21.7 us
    unnamed x1, local copies, waits for them, and re-layouts  0.63 us

profile of v6, /device:TPU:97, one launch (start us, length us, event | category | flops | bytes accessed | tf_op | source)
XLA Modules:
  0.0 22.3 jit_solution(11067770733020567880)
XLA Ops:
  0.0 21.7 %correlate.1 = f32[16,8,128]{2,1,0:T(8,128)S(1)} custom-call(s32[8]{0:T(128)} %refs_0_.1, bf16[1,8,4096]{2,1,0:T(8,128)(2,1)} %refs_1_.1, bf16[256,128]{1,0:T(8,128)(2,1)} %constant.8.clone.refs_2_, f32[2,128,256]{2,1,0:T(8,128)} %constant.9.clone.refs_3_, bf16[2,512,128]{2,1,0:T(8,128)(2,1)} %constant.10.clone.refs_4_, ...), custom_call_target="tpu_custom_call" | custom-call | tf_op jit(solution)/shard_map/correlate/pallas_call | solution.py:447
  21.7 0.6 %copy.8 = f32[16,8,128]{2,1,0:T(8,128)} copy(f32[16,8,128]{2,1,0:T(8,128)S(1)} %correlate.1) | data formatting | bytes 131072

commit v7 on v6

--- a/solution.py
+++ b/solution.py
@@ -349,7 +349,7 @@
     )
     before = (
         {
-            1: [row_is_in, *chip((1, SAME), (2, ACROSS), (1, ACROSS), (3, SAME))],
+            1: [row_is_in, *chip((1, SAME), (1, ACROSS), (2, ACROSS), (3, SAME))],
             4: [rest_is_in, *sums(2, 3)],
             5: [*chip((0, SAME)), *sums(5, 1)],
             6: chip(FAR, (3, ACROSS)),
@@ -357,7 +357,7 @@
             8: sums(6, 1),
         },
         {
-            1: [row_is_in, *chip((3, SAME), (2, ACROSS), (3, ACROSS), (1, SAME))],
+            1: [row_is_in, *chip((3, SAME), (3, ACROSS), (2, ACROSS), (1, SAME))],
             4: [*chip((1, ACROSS)), rest_is_in, *sums(3, 3)],
             6: [*chip((0, SAME)), *sums(1, 2), *chip((4, SAME))],
             7: [*sums(0, 1), *chip(FAR)],

time: 22.4 us -> 22.6 us (level)
  no operation moved by 1% of the time
where the time goes in v7:
time: 22.6 us; the launch traced here: 22.5 us
  Pallas kernels  21.9 us (97%)
  local copies, waits for them, and re-layouts  0.63 us (3%)
    pallas_call x1, Pallas kernels, local(): pl.pallas_call(body, out_shape=pltpu.VMEM((group, C, LAGS), jnp.float32),...  21.9 us
    unnamed x1, local copies, waits for them, and re-layouts  0.63 us

profile of v7, /device:TPU:97, one launch (start us, length us, event | category | flops | bytes accessed | tf_op | source)
XLA Modules:
  0.0 22.5 jit_solution(2151773298061453745)
XLA Ops:
  0.0 21.9 %correlate.1 = f32[16,8,128]{2,1,0:T(8,128)S(1)} custom-call(s32[8]{0:T(128)} %refs_0_.1, bf16[1,8,4096]{2,1,0:T(8,128)(2,1)} %refs_1_.1, bf16[256,128]{1,0:T(8,128)(2,1)} %constant.8.clone.refs_2_, f32[2,128,256]{2,1,0:T(8,128)} %constant.9.clone.refs_3_, bf16[2,512,128]{2,1,0:T(8,128)(2,1)} %constant.10.clone.refs_4_, ...), custom_call_target="tpu_custom_call" | custom-call | tf_op jit(solution)/shard_map/correlate/pallas_call | solution.py:447
  21.9 0.6 %copy.8 = f32[16,8,128]{2,1,0:T(8,128)} copy(f32[16,8,128]{2,1,0:T(8,128)S(1)} %correlate.1) | data formatting | bytes 131072

commit v8 on v6

--- a/solution.py
+++ b/solution.py
@@ -26,7 +26,7 @@
 MESH = pl.DeviceIdType.MESH
 SAME, ACROSS = "same", "across"
 T1, A1, HERE = "t1", "a1", "here"
-ISSUE = [(T1, ACROSS), (T1, SAME), (A1, SAME), (HERE, ACROSS)]
+ISSUE = [(T1, ACROSS), (HERE, ACROSS), (T1, SAME), (A1, SAME)]
 FAR = "far"
 PLACES = [(2, ACROSS), (1, SAME), (1, ACROSS), (3, SAME), (3, ACROSS), (0, SAME), (4, SAME), FAR]
 

time: 22.4 us -> 22.4 us (level)
  no operation moved by 1% of the time
where the time goes in v8:
time: 22.4 us; the launch traced here: 22.3 us
  Pallas kernels  21.7 us (97%)
  local copies, waits for them, and re-layouts  0.63 us (3%)
    pallas_call x1, Pallas kernels, local(): pl.pallas_call(body, out_shape=pltpu.VMEM((group, C, LAGS), jnp.float32),...  21.7 us
    unnamed x1, local copies, waits for them, and re-layouts  0.63 us

profile of v8, /device:TPU:97, one launch (start us, length us, event | category | flops | bytes accessed | tf_op | source)
XLA Modules:
  0.0 22.3 jit_solution(7887348695142855325)
XLA Ops:
  0.0 21.7 %correlate.1 = f32[16,8,128]{2,1,0:T(8,128)S(1)} custom-call(s32[8]{0:T(128)} %refs_0_.1, bf16[1,8,4096]{2,1,0:T(8,128)(2,1)} %refs_1_.1, bf16[256,128]{1,0:T(8,128)(2,1)} %constant.8.clone.refs_2_, f32[2,128,256]{2,1,0:T(8,128)} %constant.9.clone.refs_3_, bf16[2,512,128]{2,1,0:T(8,128)(2,1)} %constant.10.clone.refs_4_, ...), custom_call_target="tpu_custom_call" | custom-call | tf_op jit(solution)/shard_map/correlate/pallas_call | solution.py:447
  21.7 0.6 %copy.8 = f32[16,8,128]{2,1,0:T(8,128)} copy(f32[16,8,128]{2,1,0:T(8,128)S(1)} %correlate.1) | data formatting | bytes 131072
